TPU v7x, 128 devices: a whole 4x4x4 slice. The times are simulated.
128 devices in a mesh: section: 2 (over x_hi), row: 8 (over y, core), col: 8 (over z, x_lo).
Axes of the slice: x: 4 (x_hi: 2, x_lo: 2; x = x_hi * 2 + x_lo), y: 4, z: 4, core: 2. Of those that a mesh axis runs over, the one named last changes fastest.
Arguments:
- layer_input: bfloat16 [2, 2, 128, 8192], P('section', None, 'col', 'row'), may hold values from -6 to 6
- top_grad: bfloat16 [2, 128, 8192], P(None, 'col', 'row'), may hold values from -6 to 6
- gate_weight: bfloat16 [2, 8192, 14336], P('section', 'row', 'col'), may hold values from -0.0625 to 0.0625
- up_weight: bfloat16 [2, 8192, 14336], P('section', 'row', 'col'), may hold values from -0.0625 to 0.0625
- down_weight: bfloat16 [2, 14336, 8192], P('section', 'col', 'row'), may hold values from -0.046875 to 0.046875
- activity: int32 [2, 2, 2, 8, 14], P('section', None, None, 'col'), may hold values from 0 to 28, as said below
Outputs:
- sent_grad: bfloat16 [2, 2, 128, 8192], P('section', None, 'col', 'row')
- gate_grad: bfloat16 [2, 8192, 14336], P('section', 'row', 'col')
- up_grad: bfloat16 [2, 8192, 14336], P('section', 'row', 'col')
- down_grad: bfloat16 [2, 14336, 8192], P('section', 'col', 'row')
Inputs may be any that keep to these rules, and one draw needn't show every extreme that they name: `activity`: each list names distinct blocks below 28, then the value 28 marks empty slots up to the end; every list holds at least 3 blocks, and in every token block some column's list is full.
All inputs are finite; a program needn't handle non-finite values.
Results may differ from a plain program's by a relative error of at most 0.006.
Values may be sent and summed in bfloat16 or wider, within the bound.
A program may use at most 192 MiB of HBM per device.

v0:
```python
import jax
import jax.numpy as jnp
from jax import lax
from jax.sharding import PartitionSpec as P

BLK = 64
TB = 64


def passed_along(value, axis, steps):
    count = lax.axis_size(axis)
    initial, last = (max(0, -steps), min(count, count - steps))
    return lax.ppermute(value, axis, [(source, source + steps) for source in range(initial, last)])


def activate(gate_total, up_total, grad_total, keep_mask):
    positive = jnp.maximum(gate_total, 0.0)
    squared = keep_mask * positive * positive
    hidden = (squared * up_total).astype(jnp.bfloat16)
    grad_up = (squared * grad_total).astype(jnp.bfloat16)
    grad_hgate = (keep_mask * 2.0 * positive * up_total * grad_total).astype(jnp.bfloat16)
    return (hidden, grad_hgate, grad_up)


def combine(gate_part, up_part, grad_part, keep_mask):
    gate_total, up_total, grad_total = lax.psum((gate_part, up_part, grad_part), "row")
    hidden, grad_hgate, grad_up = activate(gate_total, up_total, grad_total, keep_mask)
    return (hidden, grad_hgate, grad_up)


def shards(layer_input, top_grad, gate_weight, up_weight, down_weight, activity):
    sections = lax.axis_size("section")
    section_pos = lax.axis_index("section")
    inputs_all = layer_input[0]
    w_gate = gate_weight[0]
    w_up = up_weight[0]
    w_down = down_weight[0]
    lists_all = activity[0, :, :, 0, :]
    micro_count = inputs_all.shape[0]
    block_total = w_gate.shape[1] // BLK
    sum_gate = jnp.zeros(w_gate.shape, jnp.float32)
    sum_up = jnp.zeros(w_up.shape, jnp.float32)
    sum_down = jnp.zeros(w_down.shape, jnp.float32)
    sent = jnp.zeros(layer_input.shape, jnp.bfloat16)
    received = jnp.zeros(inputs_all.shape[1:], jnp.bfloat16)
    for tick_number in range(micro_count + sections - 1):
        micro_pos = tick_number - (sections - 1 - section_pos)
        usable = jnp.logical_and(micro_pos >= 0, micro_pos < micro_count)
        chosen = jnp.clip(micro_pos, 0, micro_count - 1)
        active_flag = usable.astype(jnp.float32)
        local_input = lax.dynamic_index_in_dim(inputs_all, chosen, 0, keepdims=False)
        top_local = lax.dynamic_index_in_dim(top_grad, chosen, 0, keepdims=False)
        grad_in = jnp.where(section_pos == sections - 1, top_local, received)
        rows_input, rows_grad = (
            lax.all_gather(local_input, "col", axis=0, tiled=True),
            lax.all_gather(grad_in, "col", axis=0, tiled=True),
        )
        block_list = lax.dynamic_index_in_dim(lists_all, chosen, 0, keepdims=False)
        tokens = rows_input.shape[0]
        block_count = tokens // TB
        blocks = jnp.arange(block_total, dtype=jnp.int32)
        block_on = (
            jnp.any(block_list[:, :, None] == blocks[None, None, :], axis=1).astype(jnp.float32)
            * active_flag
        )
        keep_mask = jnp.broadcast_to(
            block_on[:, None, :, None], (block_count, TB, block_total, BLK)
        ).reshape(tokens, block_total * BLK)
        gate_part = jnp.dot(rows_input, w_gate, preferred_element_type=jnp.float32)
        up_part = jnp.dot(rows_input, w_up, preferred_element_type=jnp.float32)
        grad_part = jnp.einsum("td,fd->tf", rows_grad, w_down, preferred_element_type=jnp.float32)
        hidden, grad_hgate, grad_up = combine(gate_part, up_part, grad_part, keep_mask)
        sum_gate = sum_gate + jnp.einsum(
            "td,tf->df", rows_input, grad_hgate, preferred_element_type=jnp.float32
        )
        sum_up = sum_up + jnp.einsum(
            "td,tf->df", rows_input, grad_up, preferred_element_type=jnp.float32
        )
        sum_down = sum_down + jnp.einsum(
            "tf,td->fd", hidden, rows_grad, preferred_element_type=jnp.float32
        )
        partial_back = jnp.einsum(
            "tf,df->td", grad_hgate, w_gate, preferred_element_type=jnp.float32
        )
        partial_back = partial_back + jnp.einsum(
            "tf,df->td", grad_up, w_up, preferred_element_type=jnp.float32
        )
        summed = lax.psum_scatter(partial_back, "col", scatter_dimension=0, tiled=True)
        handed = (grad_in.astype(jnp.float32) + summed).astype(jnp.bfloat16)
        written = lax.dynamic_update_slice(sent, handed[None, None], (0, chosen, 0, 0))
        sent = jnp.where(usable, written, sent)
        received = passed_along(handed, "section", -1)
    return (
        sent,
        sum_gate.astype(jnp.bfloat16)[None],
        sum_up.astype(jnp.bfloat16)[None],
        sum_down.astype(jnp.bfloat16)[None],
    )


def solution(mesh):
    in_specs = (
        P("section", None, "col", "row"),
        P(None, "col", "row"),
        P("section", "row", "col"),
        P("section", "row", "col"),
        P("section", "col", "row"),
        P("section", None, None, "col", None),
    )
    out_specs = (
        P("section", None, "col", "row"),
        P("section", "row", "col"),
        P("section", "row", "col"),
        P("section", "col", "row"),
    )
    return jax.shard_map(shards, mesh=mesh, in_specs=in_specs, out_specs=out_specs, check_vma=False)
```

profile of v0, /device:TPU:1, one launch (start us, length us, event | category | flops | bytes accessed | tf_op | source)
XLA Modules:
  0.0 496.5 jit_solution(2840908331639609842)
XLA Ops:
  7.2 1.6 constant_dynamic-slice_fusion
  8.8 25.3 %all-gather = bf16[1,1,128,1024]{3,2,1,0:T(8,128)(2,1)S(1)} all-gather(bf16[1,1,16,1024]{3,2,1,0:T(8,128)(2,1)S(1)} %get-tuple-element.24), channel_id=2, replica_groups=mesh['section'=2,'row'=8,'col'=8] {'col'}, dimensions={2}, use_global_device_ids=true | all-gather | bytes 294912 | tf_op jit(solution)/shard_map/all_gather | solution.py:55
  34.1 3.6 fusion.16
  37.8 1.6 fusion.28
  39.3 22.8 %all-gather.1 = bf16[1,128,1024]{2,1,0:T(8,128)(2,1)S(1)} all-gather(bf16[1,16,1024]{2,1,0:T(8,128)(2,1)S(1)} %dynamic-slice_select_fusion), channel_id=3, replica_groups=mesh['section'=2,'row'=8,'col'=8] {'col'}, dimensions={1}, use_global_device_ids=true | all-gather | bytes 294912 | tf_op jit(solution)/shard_map/all_gather | solution.py:56
  62.9 2.3 fusion.4
  67.3 76.5 %all-reduce.11.cloned.1.call-done = (f32[128,1792]{1,0:T(8,128)}, f32[128,1792]{1,0:T(8,128)}, f32[128,1792]{1,0:T(8,128)}) async-done(((f32[128,1792]{1,0:T(8,128)}, f32[128,1792]{1,0:T(8,128)}, f32[128,1792]{1,0:T(8,128)}), (f32[128,1792]{1,0:T(8,128)}, f32[128,1792]{1,0:T(8,128)}, f32[128,1792]{1,0:T(8,128)})) %all-reduce.11.cloned.1.call-update) | async-done | bytes 2752528 | tf_op jit(solution)/shard_map/psum | solution.py:26
  143.8 2.1 multiply_convert_fusion.8
  146.7 1.3 fusion.14
  148.1 2.1 fusion.33
  150.3 24.7 %all-gather.2 = bf16[1,1,128,1024]{3,2,1,0:T(8,128)(2,1)S(1)} all-gather(bf16[1,1,16,1024]{3,2,1,0:T(8,128)(2,1)S(1)} %get-tuple-element.25), channel_id=4, replica_groups=mesh['section'=2,'row'=8,'col'=8] {'col'}, dimensions={2}, use_global_device_ids=true | all-gather | bytes 294912 | tf_op jit(solution)/shard_map/all_gather | solution.py:55
  175.0 3.7 fusion.12
  178.7 7.7 %reduce-scatter.4.cloned.1.call-done = f32[16,1024]{1,0:T(8,128)} async-done(((f32[128,1024]{1,0:T(8,128)}), f32[16,1024]{1,0:T(8,128)}) %reduce-scatter.4.cloned.1.call-update) | async-done | bytes 65552 | tf_op jit(solution)/shard_map/reduce_scatter | solution.py:88
  187.4 1.4 collective-permute-start
  188.9 3.6 fusion.24
  193.8 22.3 %all_gather.21 = bf16[128,1024]{1,0:T(8,128)(2,1)S(1)} all-gather(bf16[16,1024]{1,0:T(8,128)(2,1)S(1)} %bitcast_select_fusion.2), channel_id=1, replica_groups=mesh['section'=2,'row'=8,'col'=8] {'col'}, dimensions={0}, use_global_device_ids=true | all-gather | bytes 294912 | tf_op jit(solution)/shard_map/all_gather | solution.py:56
  216.1 2.3 fusion.2
  218.8 1.8 broadcast_in_dim.52
  220.6 2.5 reshape.49
  223.5 1.8 broadcast_in_dim.54
  225.3 3.1 reshape.50
  228.4 1.5 copy.23
  229.9 22.5 %all-gather.3 = bf16[1,1,128,1024]{3,2,1,0:T(8,128)(2,1)S(1)} all-gather(bf16[1,1,16,1024]{3,2,1,0:T(8,128)(2,1)} %get-tuple-element.23), channel_id=5, replica_groups=mesh['section'=2,'row'=8,'col'=8] {'col'}, dimensions={2}, use_global_device_ids=true | all-gather | bytes 294912 | tf_op jit(solution)/shard_map/all_gather | solution.py:55
  252.4 42.2 %all-reduce.9.cloned.1.call-done = (f32[128,1792]{1,0:T(8,128)}, f32[128,1792]{1,0:T(8,128)}, f32[128,1792]{1,0:T(8,128)}) async-done(((f32[128,1792]{1,0:T(8,128)}, f32[128,1792]{1,0:T(8,128)}, f32[128,1792]{1,0:T(8,128)}), (f32[128,1792]{1,0:T(8,128)}, f32[128,1792]{1,0:T(8,128)}, f32[128,1792]{1,0:T(8,128)})) %all-reduce.9.cloned.1.call-update) | async-done | bytes 2752528 | tf_op jit(solution)/shard_map/psum | solution.py:26
  294.6 2.1 multiply_convert_fusion.6
  297.5 1.3 fusion.10
  298.9 2.1 fusion.36
  301.1 3.8 fusion.20
  304.9 1.6 fusion.8
  306.5 4.1 fusion.42
  310.6 25.4 %reduce-scatter.6.cloned.1.call-done = f32[16,1024]{1,0:T(8,128)} async-done(((f32[128,1024]{1,0:T(8,128)}), f32[16,1024]{1,0:T(8,128)}) %reduce-scatter.6.cloned.1.call-update) | async-done | bytes 65552 | tf_op jit(solution)/shard_map/reduce_scatter | solution.py:88
  336.0 1.5 fusion.66
  337.5 1.5 collective-permute-start.1
  339.0 5.2 %fusion.56 = f32[1024,1792]{1,0:T(8,128)} fusion(bf16[128,1792]{1,0:T(8,128)(2,1)} %copy-done.19, bf16[1,1,128,1024]{3,2,1,0:T(8,128)(2,1)S(1)} %all-gather), kind=kOutput, calls=%fused_computation.65 | convolution fusion | flops 469762048 | bytes 8060928 | tf_op jit(solution)/shard_map/td,tf->df/dot_general | solution.py:76
  344.2 22.4 %all_gather.23 = bf16[128,1024]{1,0:T(8,128)(2,1)S(1)} all-gather(bf16[16,1024]{1,0:T(8,128)(2,1)S(1)} %bitcast_select_fusion), channel_id=1, replica_groups=mesh['section'=2,'row'=8,'col'=8] {'col'}, dimensions={0}, use_global_device_ids=true | all-gather | bytes 294912 | tf_op jit(solution)/shard_map/all_gather | solution.py:56
  366.6 2.3 fusion
  369.2 4.1 fusion.58
  373.3 4.1 fusion.48
  377.5 4.2 fusion.50
  381.7 4.1 fusion.43
  385.8 60.9 %all-reduce.7.cloned.1.call-done = (f32[128,1792]{1,0:T(8,128)}, f32[128,1792]{1,0:T(8,128)}, f32[128,1792]{1,0:T(8,128)}) async-done(((f32[128,1792]{1,0:T(8,128)}, f32[128,1792]{1,0:T(8,128)}, f32[128,1792]{1,0:T(8,128)}), (f32[128,1792]{1,0:T(8,128)}, f32[128,1792]{1,0:T(8,128)}, f32[128,1792]{1,0:T(8,128)})) %all-reduce.7.cloned.1.call-update) | async-done | bytes 2752528 | tf_op jit(solution)/shard_map/psum | solution.py:26
  446.7 2.2 multiply_convert_fusion.4
  449.6 1.3 fusion.6
  451.0 2.1 fusion.39
  453.2 8.5 %fusion.31 = bf16[1,1024,1792]{2,1,0:T(8,128)(2,1)} fusion(bf16[128,1792]{1,0:T(8,128)(2,1)} %copy-done.26, f32[1024,1792]{1,0:T(8,128)} %fusion.56, f32[1024,1792]{1,0:T(8,128)} %fusion.48, bf16[1,1,128,1024]{3,2,1,0:T(8,128)(2,1)S(1)} %all-gather.3), kind=kOutput, calls=%fused_computation.34 | convolution fusion | flops 475267072 | bytes 19070976 | tf_op jit(solution)/shard_map/td,tf->df/dot_general | solution.py:76
  461.8 7.0 %fusion.30 = bf16[1,1024,1792]{2,1,0:T(8,128)(2,1)} fusion(bf16[128,1792]{1,0:T(8,128)(2,1)S(1)} %copy-done.25, f32[1024,1792]{1,0:T(8,128)S(1)} %bitcast.127, f32[1024,1792]{1,0:T(8,128)} %fusion.50, bf16[1,1,128,1024]{3,2,1,0:T(8,128)(2,1)S(1)} %all-gather.3), kind=kOutput, calls=%fused_computation.33 | convolution fusion | flops 475267072 | bytes 19070976 | tf_op jit(solution)/shard_map/td,tf->df/dot_general | solution.py:73
  469.5 3.0 fusion.32
  472.4 15.7 %reduce-scatter.8.cloned.1.call-done = f32[16,1024]{1,0:T(8,128)} async-done(((f32[128,1024]{1,0:T(8,128)}), f32[16,1024]{1,0:T(8,128)}) %reduce-scatter.8.cloned.1.call-update) | async-done | bytes 65552 | tf_op jit(solution)/shard_map/reduce_scatter | solution.py:88
  (137 shorter events, 11.3 us)
Async XLA Ops:
  7.2 136.6 %all-reduce.11.cloned.1.call-start = ((), (), s32[]{:S(2)}) async-start(), calls=%async_computation.8 | async-start | bytes 5505024 | tf_op jit(solution)/shard_map/psum | solution.py:26
  7.2 30.5 %copy-start.4 = (bf16[1,1024,1792]{2,1,0:T(8,128)(2,1)S(1)}, bf16[1,1024,1792]{2,1,0:T(8,128)(2,1)}, u32[]{:S(2)}) copy-start(bf16[1,1024,1792]{2,1,0:T(8,128)(2,1)} %param.8) | copy-start | bytes 11010052
  34.1 5.2 %copy-start.38 = (bf16[2,16,1024]{2,1,0:T(8,128)(2,1)S(1)}, bf16[2,16,1024]{2,1,0:T(8,128)(2,1)}, u32[]{:S(2)}) copy-start(bf16[2,16,1024]{2,1,0:T(8,128)(2,1)} %param.7) | copy-start | bytes 196612
  37.7 25.1 %copy-start.8 = (bf16[1,1792,1024]{2,1,0:T(8,128)(2,1)S(1)}, bf16[1,1792,1024]{2,1,0:T(8,128)(2,1)}, u32[]{:S(2)}) copy-start(bf16[1,1792,1024]{2,1,0:T(8,128)(2,1)} %param.10) | copy-start | bytes 11010052
  65.1 121.3 %reduce-scatter.4.cloned.1.call-start = ((), (), s32[]{:S(2)}) async-start(), calls=%async_computation.3 | async-start | bytes 589824 | tf_op jit(solution)/shard_map/reduce_scatter | solution.py:88
  143.8 2.9 copy-start
  143.8 4.3 copy-start.5
  145.9 4.3 copy-start.17
  146.0 4.3 copy-start.19
  150.2 144.4 %all-reduce.9.cloned.1.call-start = ((), (), s32[]{:S(2)}) async-start(), calls=%async_computation.7 | async-start | bytes 5505024 | tf_op jit(solution)/shard_map/psum | solution.py:26
  186.4 29.6 %copy-start.9 = (bf16[1,1792,1024]{2,1,0:T(8,128)(2,1)S(1)}, bf16[1,1792,1024]{2,1,0:T(8,128)(2,1)}, u32[]{:S(2)}) copy-start(bf16[1,1792,1024]{2,1,0:T(8,128)(2,1)} %param.10) | copy-start | bytes 11010052
  187.4 31.4 %copy-start.40 = (bf16[1,2,16,1024]{3,2,1,0:T(8,128)(2,1)}, bf16[1,2,16,1024]{3,2,1,0:T(8,128)(2,1)S(1)}, u32[]{:S(2)}) copy-start(bf16[1,2,16,1024]{3,2,1,0:T(8,128)(2,1)S(1)} %get-tuple-element.15) | copy-start | bytes 196612
  187.4 6.3 %collective-permute-start = (bf16[16,1024]{1,0:T(8,128)(2,1)S(1)}, bf16[16,1024]{1,0:T(8,128)(2,1)S(1)}, u32[]{:S(2)}, u32[]{:S(2)}) collective-permute-start(bf16[16,1024]{1,0:T(8,128)(2,1)S(1)} %get-tuple-element.16), channel_id=1, source_target_pairs={{64,0},{65,1},{66,2},{67,3},{68,4},{69,5},{70,6},{71,7},{72,8},{73... | collective-permute-start | bytes 98312 | tf_op jit(solution)/shard_map/ppermute | solution.py:13
  193.8 24.6 %copy-start.37 = (bf16[16,1024]{1,0:T(8,128)(2,1)}, bf16[16,1024]{1,0:T(8,128)(2,1)S(1)}, u32[]{:S(2)}) copy-start(bf16[16,1024]{1,0:T(8,128)(2,1)S(1)} %bitcast_select_fusion.2) | copy-start | bytes 98308
  218.4 117.7 %reduce-scatter.6.cloned.1.call-start = ((), (), s32[]{:S(2)}) async-start(), calls=%async_computation.4 | async-start | bytes 589824 | tf_op jit(solution)/shard_map/reduce_scatter | solution.py:88
  229.9 216.8 %copy-start.11 = (f32[128,1792]{1,0:T(8,128)}, f32[128,1792]{1,0:T(8,128)S(1)}, u32[]{:S(2)}) copy-start(f32[128,1792]{1,0:T(8,128)S(1)} %copy.23) | copy-start | bytes 2752516
  294.6 2.9 copy-start.1
  294.6 4.3 copy-start.6
  301.1 145.6 %all-reduce.7.cloned.1.call-start = ((), (), s32[]{:S(2)}) async-start(), calls=%async_computation.6 | async-start | bytes 5505024 | tf_op jit(solution)/shard_map/psum | solution.py:26
  301.1 3.8 copy-start.2
  301.1 5.4 %copy-start.13 = (f32[128,1792]{1,0:T(8,128)S(1)}, f32[128,1792]{1,0:T(8,128)}, u32[]{:S(2)}) copy-start(f32[128,1792]{1,0:T(8,128)} %get-tuple-element.11) | copy-start | bytes 2752516
  301.1 5.4 %copy-start.14 = (f32[128,1792]{1,0:T(8,128)S(1)}, f32[128,1792]{1,0:T(8,128)}, u32[]{:S(2)}) copy-start(f32[128,1792]{1,0:T(8,128)} %get-tuple-element.12) | copy-start | bytes 2752516
  301.1 5.4 %copy-start.30 = (bf16[1,128,1024]{2,1,0:T(8,128)(2,1)S(1)}, bf16[1,128,1024]{2,1,0:T(8,128)(2,1)}, u32[]{:S(2)}) copy-start(bf16[1,128,1024]{2,1,0:T(8,128)(2,1)} %copy-done.29) | copy-start | bytes 786436
  337.5 6.7 %copy-start.39 = (bf16[2,16,1024]{2,1,0:T(8,128)(2,1)S(1)}, bf16[2,16,1024]{2,1,0:T(8,128)(2,1)}, u32[]{:S(2)}) copy-start(bf16[2,16,1024]{2,1,0:T(8,128)(2,1)} %param.7) | copy-start | bytes 196612
  337.5 29.1 %copy-start.10 = (bf16[1,1792,1024]{2,1,0:T(8,128)(2,1)S(1)}, bf16[1,1792,1024]{2,1,0:T(8,128)(2,1)}, u32[]{:S(2)}) copy-start(bf16[1,1792,1024]{2,1,0:T(8,128)(2,1)} %param.10) | copy-start | bytes 11010052
  337.5 6.7 %collective-permute-start.1 = (bf16[16,1024]{1,0:T(8,128)(2,1)S(1)}, bf16[16,1024]{1,0:T(8,128)(2,1)S(1)}, u32[]{:S(2)}, u32[]{:S(2)}) collective-permute-start(bf16[16,1024]{1,0:T(8,128)(2,1)S(1)} %get-tuple-element.14), channel_id=1, source_target_pairs={{64,0},{65,1},{66,2},{67,3},{68,4},{69,5},{70,6},{71,7},{72,8},{73... | collective-permute-start | bytes 98312 | tf_op jit(solution)/shard_map/ppermute | solution.py:13
  344.2 24.7 %copy-start.35 = (bf16[16,1024]{1,0:T(8,128)(2,1)}, bf16[16,1024]{1,0:T(8,128)(2,1)S(1)}, u32[]{:S(2)}) copy-start(bf16[16,1024]{1,0:T(8,128)(2,1)S(1)} %bitcast_select_fusion) | copy-start | bytes 98308
  368.9 4.4 copy-start.23
  368.9 119.2 %reduce-scatter.8.cloned.1.call-start = ((), (), s32[]{:S(2)}) async-start(), calls=%async_computation.5 | async-start | bytes 589824 | tf_op jit(solution)/shard_map/reduce_scatter | solution.py:88
  373.3 4.2 copy-start.21
  377.5 4.2 copy-start.15
  377.5 4.2 copy-start.16
  377.5 4.2 copy-start.32
  446.7 2.9 copy-start.3
  446.7 4.3 copy-start.7
  451.0 10.7 %slice-start.4 = ((s8[7340032]{0:T(1024)(128)(4,1)}), s8[3145728]{0:T(1024)(128)(4,1)S(1)}, s32[]{:S(2)}) async-start(s8[7340032]{0:T(1024)(128)(4,1)} %bitcast.126), calls=%async_computation.13 | async-start | bytes 6291456
  453.2 8.5 %slice-start.5 = ((s8[7340032]{0:T(1024)(128)(4,1)}), s8[4194304]{0:T(1024)(128)(4,1)S(1)}, s32[]{:S(2)}) async-start(s8[7340032]{0:T(1024)(128)(4,1)} %bitcast.126), calls=%async_computation.14 | async-start | bytes 8388608
  453.2 8.5 %copy-start.25 = (bf16[128,1792]{1,0:T(8,128)(2,1)S(1)}, bf16[128,1792]{1,0:T(8,128)(2,1)}, u32[]{:S(2)}) copy-start(bf16[128,1792]{1,0:T(8,128)(2,1)} %copy-done.24) | copy-start | bytes 1376260
  453.2 15.6 %slice-start = ((s8[7340032]{0:T(1024)(128)(4,1)}), s8[4194304]{0:T(1024)(128)(4,1)S(1)}, s32[]{:S(2)}) async-start(s8[7340032]{0:T(1024)(128)(4,1)} %bitcast.122), calls=%async_computation.9 | async-start | bytes 8388608
  453.2 15.6 %slice-start.2 = ((s8[7340032]{0:T(1024)(128)(4,1)}), s8[4194304]{0:T(1024)(128)(4,1)S(1)}, s32[]{:S(2)}) async-start(s8[7340032]{0:T(1024)(128)(4,1)} %bitcast.124), calls=%async_computation.11 | async-start | bytes 8388608
  461.7 7.1 %slice-start.1 = ((s8[7340032]{0:T(1024)(128)(4,1)}), s8[3145728]{0:T(1024)(128)(4,1)S(1)}, s32[]{:S(2)}) async-start(s8[7340032]{0:T(1024)(128)(4,1)} %bitcast.122), calls=%async_computation.10 | async-start | bytes 6291456
  461.7 7.0 %slice-start.3 = ((s8[7340032]{0:T(1024)(128)(4,1)}), s8[3145728]{0:T(1024)(128)(4,1)S(1)}, s32[]{:S(2)}) async-start(s8[7340032]{0:T(1024)(128)(4,1)} %bitcast.124), calls=%async_computation.12 | async-start | bytes 6291456
  461.7 7.0 %copy-start.12 = (f32[128,1792]{1,0:T(8,128)S(1)}, f32[128,1792]{1,0:T(8,128)}, u32[]{:S(2)}) copy-start(f32[128,1792]{1,0:T(8,128)} %copy-done.11) | copy-start | bytes 2752516
  461.7 7.0 %copy-start.27 = (f32[128,1792]{1,0:T(8,128)S(1)}, f32[128,1792]{1,0:T(8,128)}, u32[]{:S(2)}) copy-start(f32[128,1792]{1,0:T(8,128)} %get-tuple-element.5) | copy-start | bytes 2752516
  461.7 7.5 %copy-start.28 = (f32[128,1792]{1,0:T(8,128)S(1)}, f32[128,1792]{1,0:T(8,128)}, u32[]{:S(2)}) copy-start(f32[128,1792]{1,0:T(8,128)} %get-tuple-element.6) | copy-start | bytes 2752516
  461.7 7.7 %copy-start.34 = (bf16[128,1024]{1,0:T(8,128)(2,1)S(1)}, bf16[128,1024]{1,0:T(8,128)(2,1)}, u32[]{:S(2)}) copy-start(bf16[128,1024]{1,0:T(8,128)(2,1)} %copy-done.33) | copy-start | bytes 786436
  469.4 18.7 %copy-start.36 = (bf16[16,1024]{1,0:T(8,128)(2,1)S(1)}, bf16[16,1024]{1,0:T(8,128)(2,1)}, u32[]{:S(2)}) copy-start(bf16[16,1024]{1,0:T(8,128)(2,1)} %copy-done.35) | copy-start | bytes 98308
  469.4 18.7 %copy-start.41 = (bf16[1,2,16,1024]{3,2,1,0:T(8,128)(2,1)S(1)}, bf16[1,2,16,1024]{3,2,1,0:T(8,128)(2,1)}, u32[]{:S(2)}) copy-start(bf16[1,2,16,1024]{3,2,1,0:T(8,128)(2,1)} %get-tuple-element.13) | copy-start | bytes 196612
  (10 other events, 18.9 us)
Sparse Core Ops, SparseCore 0:
  65.3 78.4 all-reduce.10
  150.4 35.9 reduce-scatter.3
  218.5 76.1 all-reduce.8
  301.2 34.7 reduce-scatter.5
  369.1 77.5 all-reduce.6
  453.3 34.7 reduce-scatter.7
where the time goes:
time: 501 us; the launch traced here: 496 us
  waiting for transfers between devices  230 us (46%)
  blocking collectives  140 us (28%)
  matrix products  79.1 us (16%)
  local copies, waits for them, and re-layouts  19.2 us (4%)
  between operations  14.6 us (3%)
  other arithmetic  10.1 us (2%)
    psum x3, waiting for transfers between devices, combine(): lax.psum((gate_part, up_part, grad_part), 'row')  180 us
    all_gather x3, blocking collectives, shards(): lax.all_gather(local_input, 'col', axis=0, tiled=True)  72.5 us
    all_gather x3, blocking collectives, shards(): lax.all_gather(grad_in, 'col', axis=0, tiled=True)  67.5 us
    reduce_scatter x3, waiting for transfers between devices, shards(): lax.psum_scatter(partial_back, 'col', scatter_dimension=0, tiled=True)  48.8 us
    dot_general x3, matrix products, shards(): jnp.einsum('td,tf->df', rows_input, grad_up, preferred_element_type=jnp.f...  17.8 us
    dot_general x3, matrix products, shards(): jnp.einsum('td,tf->df', rows_input, grad_hgate, preferred_element_type=jn...  15.2 us
    dot_general x3, matrix products, shards(): jnp.einsum('tf,td->fd', hidden, rows_grad, preferred_element_type=jnp.flo...  11.2 us
  transfers between devices with their start and end apart: 8, of which 7 were waited for; matrix products, arithmetic and copies ran while one was open for 14% of the time, Pallas kernels for 0%

commit v1 on v0

v1 whole, which is shorter than its diff:
```python
import functools

import jax
import jax.numpy as jnp
from jax import lax
from jax.experimental import pallas as pl
from jax.experimental.pallas import tpu as pltpu
from jax.sharding import PartitionSpec as P

MESH = pl.DeviceIdType.MESH
F32, BF16 = jnp.float32, jnp.bfloat16
NT = (((1,), (1,)), ((), ()))
TN = (((0,), (0,)), ((), ()))

BLK = 64
TOK = 128
DL = 1024
FL = 1792
NBLK = 28
SLOTS = 14
HALF = 7
COL_STEPS = ((1, 0), (3, 0), (2, 0), (0, 1), (1, 1), (3, 1), (2, 1))


def relay_kernel(
    x_hbm, top_hbm, wg_hbm, wu_hbm, wd_hbm, act_ref,
    sent_hbm, xall_hbm, dyall_hbm, hid_hbm, gh_hbm, gu_hbm,
    xs, dys, wg, wu, wd, dn, ps, pr, yo, ys, yr,
    agb0, agb1, agh0, agh1, hid, gh, gu, dxf, dxs, rr, sentv, inv_y, inv_i,
    w_sem, own_sem, out_sem,
    x_s, x_r, dy_s, dy_r, pair_s, pair_r, y_s, y_r,
    ag_s, ag_r, agp_s, agp_r, hg_s, hg_r, hgp_s, hgp_r, rs_s, rs_r, hand_s, hand_r,
):
    agb, agh = (agb0, agb1), (agh0, agh1)
    sec, row, col = (lax.axis_index(a) for a in ("section", "row", "col"))
    y, k = row // 2, lax.rem(row, 2)
    z, xl = col // 2, lax.rem(col, 2)
    last = sec == 1

    def at_col(step, sign=1):
        dz, dx = step
        zz = lax.rem(z + (dz if sign > 0 else 4 - dz), 4)
        return zz * 2 + ((1 - xl) if dx else xl)

    def col_dev(step, sign=1):
        return (sec, row, at_col(step, sign))

    def y_at(d):
        return lax.rem(y + d, 4)

    def y_dev(d):
        return (sec, y_at(d) * 2 + k, col)

    pair = (sec, 2 * y + 1 - k, col)
    relay = (1 - sec, row, 2 * z + 1 - xl)

    def remote(src, dst, ss, rs, dev):
        return pltpu.make_async_remote_copy(
            src_ref=src, dst_ref=dst, send_sem=ss, recv_sem=rs, device_id=dev, device_id_type=MESH
        )

    def rows16(c):
        return pl.ds(pl.multiple_of(c * 16, 16), 16)

    weights = [
        pltpu.make_async_copy(src.at[0], dst, w_sem.at[i])
        for i, (src, dst) in enumerate(((wg_hbm, wg), (wu_hbm, wu), (wd_hbm, wd)))
    ]
    own_x = [
        pltpu.make_async_copy(x_hbm.at[0, m], xs.at[m, rows16(col)], own_sem.at[m]) for m in range(2)
    ]
    own_dy = [
        pltpu.make_async_copy(top_hbm.at[m], dys.at[m, rows16(col)], own_sem.at[2 + m])
        for m in range(2)
    ]
    for c in own_x:
        c.start()

    @pl.when(last)
    def _():
        for c in own_dy:
            c.start()

    for c in weights:
        c.start()

    barrier = pltpu.get_barrier_semaphore()
    partners = [col_dev(s) for s in COL_STEPS] + [y_dev(d) for d in (1, 2, 3)] + [pair, relay]
    for dev in partners:
        pl.semaphore_signal(barrier, inc=1, device_id=dev, device_id_type=MESH)
    pl.semaphore_wait(barrier, len(partners))

    def send_x(m, i):
        return remote(x_hbm.at[0, m], xs.at[m, rows16(col)], x_s.at[m, i], x_r.at[m, i], col_dev(COL_STEPS[i]))

    def recv_x(m, i):
        block = xs.at[m, rows16(at_col(COL_STEPS[i], -1))]
        return remote(block, block, x_s.at[m, i], x_r.at[m, i], col_dev(COL_STEPS[i]))

    def dy_block(c):
        flipped = c + 1 - 2 * lax.rem(c, 2)
        return jnp.where(last, c, flipped)

    def send_dy(m, i, src):
        block = rows16(dy_block(col))
        return remote(src, dys.at[m, block], dy_s.at[m, i], dy_r.at[m, i], col_dev(COL_STEPS[i]))

    def recv_dy(m, i):
        block = dys.at[m, rows16(dy_block(at_col(COL_STEPS[i], -1)))]
        return remote(block, block, dy_s.at[m, i], dy_r.at[m, i], col_dev(COL_STEPS[i]))

    MATS = ((0, 2), (2, 1))

    def pair_copy(m, j):
        lo, n = MATS[j]
        return remote(
            ps.at[m, pl.ds(lo, n)], pr.at[m, pl.ds(lo, n)], pair_s.at[m, j], pair_r.at[m, j], pair
        )

    def y_copy(m, j, d):
        lo, n = MATS[j]
        return remote(
            ys.at[m, d - 1, pl.ds(lo, n)], yr.at[m, d - 1, pl.ds(lo, n)],
            y_s.at[m, j, d - 1], y_r.at[m, j, d - 1], y_dev(d),
        )

    def ag_y(buf, ss, rs, m, d):
        return remote(buf[m].at[y, k], buf[m].at[y, k], ss.at[m, d - 1], rs.at[m, d - 1], y_dev(d))

    def ag_y_recv(buf, ss, rs, m, d):
        block = buf[m].at[y_at(4 - d), k]
        return remote(block, block, ss.at[m, d - 1], rs.at[m, d - 1], y_dev(d))

    def ag_pair(buf, ss, rs, m, d):
        block = buf[m].at[y_at(4 - d) if d else y, k]
        return remote(block, block, ss.at[m, d], rs.at[m, d], pair)

    def ag_pair_recv(buf, ss, rs, m, d):
        block = buf[m].at[y_at(4 - d) if d else y, 1 - k]
        return remote(block, block, ss.at[m, d], rs.at[m, d], pair)

    def rs_copy(m, i):
        return remote(
            dxs.at[m, rows16(at_col(COL_STEPS[i]))], rr.at[m, i], rs_s.at[m, i], rs_r.at[m, i],
            col_dev(COL_STEPS[i]),
        )

    def hand_copy(m):
        return remote(sentv.at[m], dys.at[m, rows16(col)], hand_s.at[m], hand_r.at[m], relay)

    def hand_recv(m):
        block = dys.at[m, rows16(dy_block(col))]
        return remote(block, block, hand_s.at[m], hand_r.at[m], relay)

    outs = [
        (xs, xall_hbm), (dys, dyall_hbm), (hid, hid_hbm), (gh, gh_hbm), (gu, gu_hbm), (sentv, sent_hbm)
    ]

    def out_copy(j, m):
        src, dst = outs[j]
        if j == 5:
            return pltpu.make_async_copy(src.at[m], dst.at[0, m], out_sem.at[j, m])
        return pltpu.make_async_copy(src.at[m], dst.at[m], out_sem.at[j, m])

    left = lax.broadcasted_iota(jnp.int32, (32, 128), 1) < 64
    left16 = lax.broadcasted_iota(jnp.int32, (16, 128), 1) < 64

    def lay_out(acc, m, mat, j):
        for tb in range(2):
            for h in range(2):
                lo = acc[64 * tb : 64 * tb + 32, 128 * h : 128 * h + 128]
                hi = acc[64 * tb + 32 : 64 * tb + 64, 128 * h : 128 * h + 128]
                dn[m, mat, tb, 4 * j + 2 * h] = jnp.where(left, lo, pltpu.roll(hi, 64, 1))
                dn[m, mat, tb, 4 * j + 2 * h + 1] = jnp.where(left, pltpu.roll(lo, 64, 1), hi)

    def pack(m, mats):
        far = pl.ds(pl.multiple_of(16 * (1 - k), 16), 16)

        def body(i, _):
            for yy in range(4):
                tb, sh = yy // 2, yy % 2
                b = jnp.minimum(act_ref[0, m, tb, 0, sh * HALF + i], NBLK - 1)
                for mat in mats:
                    ps[m, mat, yy, i] = dn[m, mat, tb, b, far, :]
            return 0

        lax.fori_loop(0, HALF, body, 0)

    def gate_up(m):
        own_x[m].wait()
        for i in range(7):
            recv_x(m, i).wait_recv()
        if m == 0:
            weights[0].wait()
            weights[1].wait()
        out_copy(0, m).start()

        def body(j, _):
            cut = pl.ds(pl.multiple_of(j * 256, 256), 256)
            lay_out(jnp.dot(xs[m], wg[:, cut], preferred_element_type=F32), m, 0, j)
            lay_out(jnp.dot(xs[m], wu[:, cut], preferred_element_type=F32), m, 1, j)
            return 0

        lax.fori_loop(0, 7, body, 0)
        pack(m, (0, 1))
        pair_copy(m, 0).start()

    def back(m):
        if m == 0:
            weights[2].wait()
        for i in range(7):
            recv_dy(m, i).wait_recv()
        out_copy(1, m).start()

        def body(j, _):
            cut = pl.ds(pl.multiple_of(j * 256, 256), 256)
            lay_out(lax.dot_general(dys[m], wd[cut, :], NT, preferred_element_type=F32), m, 2, j)
            return 0

        lax.fori_loop(0, 7, body, 0)
        pack(m, (2,))
        pair_copy(m, 1).start()

    def reduce_pair(m, j):
        pair_copy(m, j).wait_recv()
        lo, n = MATS[j]
        near = pl.ds(pl.multiple_of(16 * k, 16), 16)
        for d in (2, 1, 3, 0):
            yy = y_at(d)
            tb, sh = yy // 2, lax.rem(yy, 2)

            def body(i, _):
                b = jnp.minimum(act_ref[0, m, tb, 0, sh * HALF + i], NBLK - 1)
                for mat in range(lo, lo + n):
                    total = dn[m, mat, tb, b, near, :] + pr[m, mat, yy, i]
                    if d:
                        ys[m, d - 1, mat, i] = total.astype(BF16)
                    else:
                        yo[m, mat, i] = total
                return 0

            lax.fori_loop(0, HALF, body, 0)
            if d:
                y_copy(m, j, d).start()

    def activate(m):
        for j in range(2):
            for d in (1, 2, 3):
                y_copy(m, j, d).wait_recv()

        def body(i, _):
            sums = []
            for mat in range(3):
                total = yo[m, mat, i]
                for d in range(3):
                    total = total + yr[m, d, mat, i].astype(F32)
                sums.append(total)
            gate, up, grad = sums
            r = jnp.maximum(gate, 0.0)
            sq = r * r
            agh[m][y, k, i] = (sq * up).astype(BF16)
            agb[m][y, k, 0, i] = (2.0 * r * up * grad).astype(BF16)
            agb[m][y, k, 1, i] = (sq * grad).astype(BF16)
            return 0

        lax.fori_loop(0, HALF, body, 0)
        for d in (2, 1, 3):
            ag_y(agb, ag_s, ag_r, m, d).start()
        ag_pair(agb, agp_s, agp_r, m, 0).start()
        for d in (2, 1, 3):
            ag_y(agh, hg_s, hg_r, m, d).start()
        ag_pair(agh, hgp_s, hgp_r, m, 0).start()

    def forward(buf, sems, m):
        ss, rs, pss, prs = sems
        for d in (1, 3, 2):
            ag_y_recv(buf, ss, rs, m, d).wait_recv()
            ag_pair(buf, pss, prs, m, d).start()

    def expand(m, tile_of, dst_of):
        def body(n, _):
            cut = pl.ds(pl.multiple_of(n * 128, 128), 128)
            for tb in range(2):
                ye, ie = inv_y[m, tb, 2 * n], inv_i[m, tb, 2 * n]
                yd, idd = inv_y[m, tb, 2 * n + 1], inv_i[m, tb, 2 * n + 1]
                for kk in range(2):
                    for src, dst in zip(tile_of, dst_of):
                        a = src(ye, kk, ie).astype(F32)
                        b = src(yd, kk, idd).astype(F32)
                        top = 64 * tb + 16 * kk
                        dst[m, top : top + 16, cut] = jnp.where(left16, a, pltpu.roll(b, 64, 1)).astype(BF16)
                        dst[m, top + 32 : top + 48, cut] = jnp.where(left16, pltpu.roll(a, 64, 1), b).astype(BF16)
            return 0

        lax.fori_loop(0, NBLK // 2, body, 0)

    def input_grad(m):
        for d in (0, 1, 3, 2):
            ag_pair_recv(agb, agp_s, agp_r, m, d).wait_recv()
        expand(
            m,
            (lambda a, b, c: agb[m][a, b, 0, c], lambda a, b, c: agb[m][a, b, 1, c]),
            (gh, gu),
        )

        def body(j, _):
            cut = pl.ds(pl.multiple_of(j * 256, 256), 256)
            part = lax.dot_general(gh[m], wg[cut, :], NT, preferred_element_type=F32)
            part = part + lax.dot_general(gu[m], wu[cut, :], NT, preferred_element_type=F32)
            dxf[m, :, cut] = part
            dxs[m, :, cut] = part.astype(BF16)
            return 0

        lax.fori_loop(0, 4, body, 0)
        for i in (6, 4, 5, 2, 3, 0, 1):
            rs_copy(m, i).start()
        out_copy(3, m).start()
        out_copy(4, m).start()

    def finish(m):
        for i in range(7):
            rs_copy(m, i).wait_recv()
        total = dys[m, rows16(col), :].astype(F32) + dxf[m, rows16(col), :]
        for i in range(7):
            total = total + rr[m, i].astype(F32)
        sentv[m] = total.astype(BF16)

        @pl.when(last)
        def _():
            hand_copy(m).start()

        out_copy(5, m).start()

    def hidden(m):
        forward(agh, (hg_s, hg_r, hgp_s, hgp_r), m)
        for d in range(4):
            ag_pair_recv(agh, hgp_s, hgp_r, m, d).wait_recv()
        expand(m, (lambda a, b, c: agh[m][a, b, c],), (hid,))
        out_copy(2, m).start()

    def take_dy(m):
        hand_recv(m).wait_recv()
        for i in (6, 4, 5, 2, 3, 0, 1):
            send_dy(m, i, dys.at[m, rows16(dy_block(col))]).start()

    def forward_grads(m):
        forward(agb, (ag_s, ag_r, agp_s, agp_r), m)

    order = (6, 4, 5, 2, 3, 0, 1)
    for m in range(2):
        for i in order:
            send_x(m, i).start()

        @pl.when(last)
        def _():
            for i in order:
                send_dy(m, i, top_hbm.at[m]).start()

    for m in range(2):
        agb[m][4] = jnp.zeros(agb[m].shape[1:], BF16)
        agh[m][4] = jnp.zeros(agh[m].shape[1:], BF16)
        for tb in range(2):
            def body(n, _):
                slot = jnp.int32(2 * SLOTS)
                for s in range(SLOTS):
                    slot = jnp.where(act_ref[0, m, tb, 0, s] == n, s, slot)
                inv_y[m, tb, n] = jnp.where(slot < SLOTS, 2 * tb + jnp.where(slot < HALF, 0, 1), 4)
                inv_i[m, tb, n] = jnp.where(
                    slot < SLOTS, jnp.where(slot < HALF, slot, slot - HALF), 0
                )
                return 0

            lax.fori_loop(0, NBLK, body, 0)

    @pl.when(last)
    def _():
        own_dy[0].wait()
        own_dy[1].wait()
        gate_up(0)
        back(0)
        reduce_pair(0, 0)
        reduce_pair(0, 1)
        gate_up(1)
        back(1)
        activate(0)
        reduce_pair(1, 0)
        reduce_pair(1, 1)
        forward_grads(0)
        input_grad(0)
        activate(1)
        forward_grads(1)
        finish(0)
        input_grad(1)
        hidden(0)
        hidden(1)
        finish(1)

    @pl.when(sec == 0)
    def _():
        gate_up(0)
        gate_up(1)
        reduce_pair(0, 0)
        reduce_pair(1, 0)
        take_dy(0)
        back(0)
        reduce_pair(0, 1)
        take_dy(1)
        activate(0)
        back(1)
        forward_grads(0)
        reduce_pair(1, 1)
        input_grad(0)
        activate(1)
        hidden(0)
        forward_grads(1)
        input_grad(1)
        finish(0)
        hidden(1)
        finish(1)

    for m in range(2):
        for i in range(7):
            send_x(m, i).wait_send()
            send_dy(m, i, dys.at[m, rows16(dy_block(col))]).wait_send()
            rs_copy(m, i).wait_send()
        for j in range(2):
            pair_copy(m, j).wait_send()
            for d in (1, 2, 3):
                y_copy(m, j, d).wait_send()
        for d in (1, 2, 3):
            ag_y(agb, ag_s, ag_r, m, d).wait_send()
            ag_y(agh, hg_s, hg_r, m, d).wait_send()
        for d in range(4):
            ag_pair(agb, agp_s, agp_r, m, d).wait_send()
            ag_pair(agh, hgp_s, hgp_r, m, d).wait_send()
        for j in range(6):
            out_copy(j, m).wait()

    @pl.when(last)
    def _():
        for m in range(2):
            hand_copy(m).wait_send()


def relay_call(layer_input, top_grad, gate_weight, up_weight, down_weight, activity):
    any_space = pl.BlockSpec(memory_space=pl.ANY)
    dma = pltpu.SemaphoreType.DMA
    vm = pltpu.VMEM
    tile = (HALF, 16, 128)
    return pl.pallas_call(
        relay_kernel,
        name="relay",
        out_shape=(
            jax.ShapeDtypeStruct((1, 2, 16, DL), BF16),
            jax.ShapeDtypeStruct((2, TOK, DL), BF16),
            jax.ShapeDtypeStruct((2, TOK, DL), BF16),
            jax.ShapeDtypeStruct((2, TOK, FL), BF16),
            jax.ShapeDtypeStruct((2, TOK, FL), BF16),
            jax.ShapeDtypeStruct((2, TOK, FL), BF16),
        ),
        in_specs=[any_space] * 5 + [pl.BlockSpec(memory_space=pltpu.SMEM)],
        out_specs=(any_space,) * 6,
        scratch_shapes=[
            vm((2, TOK, DL), BF16), vm((2, TOK, DL), BF16),
            vm((DL, FL), BF16), vm((DL, FL), BF16), vm((FL, DL), BF16),
            vm((2, 3, 2, NBLK, 32, 128), F32),
            vm((2, 3, 4) + tile, F32), vm((2, 3, 4) + tile, F32),
            vm((2, 3) + tile, F32), vm((2, 3, 3) + tile, BF16), vm((2, 3, 3) + tile, BF16),
            vm((5, 2, 2) + tile, BF16), vm((5, 2, 2) + tile, BF16),
            vm((5, 2) + tile, BF16), vm((5, 2) + tile, BF16),
            vm((2, TOK, FL), BF16), vm((2, TOK, FL), BF16), vm((2, TOK, FL), BF16),
            vm((2, TOK, DL), F32), vm((2, TOK, DL), BF16), vm((2, 7, 16, DL), BF16), vm((2, 16, DL), BF16),
            pltpu.SMEM((2, 2, NBLK), jnp.int32), pltpu.SMEM((2, 2, NBLK), jnp.int32),
            dma((3,)), dma((4,)), dma((6, 2)),
            dma((2, 7)), dma((2, 7)), dma((2, 7)), dma((2, 7)),
            dma((2, 2)), dma((2, 2)), dma((2, 2, 3)), dma((2, 2, 3)),
            dma((2, 3)), dma((2, 3)), dma((2, 4)), dma((2, 4)),
            dma((2, 3)), dma((2, 3)), dma((2, 4)), dma((2, 4)),
            dma((2, 7)), dma((2, 7)), dma((2,)), dma((2,)),
        ],
        compiler_params=pltpu.CompilerParams(
            collective_id=1, has_side_effects=True, vmem_limit_bytes=48 * 2**20
        ),
        cost_estimate=pl.CostEstimate(flops=5 * 2**30, bytes_accessed=16 * 2**20, transcendentals=0),
    )(layer_input, top_grad, gate_weight, up_weight, down_weight, activity)


def weights_kernel(x_ref, dy_ref, hid_ref, gh_ref, gu_ref, sent_ref, out_sent, og, ou, od, xt):
    @pl.when(pl.program_id(0) == 0)
    def _():
        xt[...] = x_ref[...].T
        out_sent[...] = sent_ref[...]

    og[0] = jnp.dot(xt[...], gh_ref[...], preferred_element_type=F32).astype(BF16)
    ou[0] = jnp.dot(xt[...], gu_ref[...], preferred_element_type=F32).astype(BF16)
    od[0] = lax.dot_general(hid_ref[...], dy_ref[...], TN, preferred_element_type=F32).astype(BF16)


def weights_call(x_all, dy_all, hid, gh, gu, sent):
    whole = lambda shape: pl.BlockSpec(shape, lambda j: (0,) * len(shape))
    cut = pl.BlockSpec((2 * TOK, 256), lambda j: (0, j))
    return pl.pallas_call(
        weights_kernel,
        name="weight_grads",
        grid=(FL // 256,),
        out_shape=(
            jax.ShapeDtypeStruct((1, 2, 16, DL), BF16),
            jax.ShapeDtypeStruct((1, DL, FL), BF16),
            jax.ShapeDtypeStruct((1, DL, FL), BF16),
            jax.ShapeDtypeStruct((1, FL, DL), BF16),
        ),
        in_specs=[whole((2 * TOK, DL)), whole((2 * TOK, DL)), cut, cut, cut, whole((1, 2, 16, DL))],
        out_specs=(
            whole((1, 2, 16, DL)),
            pl.BlockSpec((1, DL, 256), lambda j: (0, 0, j)),
            pl.BlockSpec((1, DL, 256), lambda j: (0, 0, j)),
            pl.BlockSpec((1, 256, DL), lambda j: (0, j, 0)),
        ),
        scratch_shapes=[pltpu.VMEM((DL, 2 * TOK), BF16)],
        compiler_params=pltpu.CompilerParams(
            dimension_semantics=("arbitrary",), vmem_limit_bytes=32 * 2**20
        ),
    )(x_all, dy_all, hid, gh, gu, sent)


def shards(layer_input, top_grad, gate_weight, up_weight, down_weight, activity):
    sent, x_all, dy_all, hid, gh, gu = relay_call(
        layer_input, top_grad, gate_weight, up_weight, down_weight, activity
    )
    flat = lambda a: a.reshape(2 * TOK, a.shape[-1])
    return weights_call(flat(x_all), flat(dy_all), flat(hid), flat(gh), flat(gu), sent)


def solution(mesh):
    in_specs = (
        P("section", None, "col", "row"),
        P(None, "col", "row"),
        P("section", "row", "col"),
        P("section", "row", "col"),
        P("section", "col", "row"),
        P("section", None, None, "col", None),
    )
    out_specs = (
        P("section", None, "col", "row"),
        P("section", "row", "col"),
        P("section", "row", "col"),
        P("section", "col", "row"),
    )
    return jax.shard_map(shards, mesh=mesh, in_specs=in_specs, out_specs=out_specs, check_vma=False)
```

time: 501 us -> 101 us (0.20)
  waiting for transfers between devices: 230 us -> 0 us
  blocking collectives: 140 us -> 0 us
  Pallas kernels: 0 us -> 97.4 us
  matrix products: 79.1 us -> 0 us
  local copies, waits for them, and re-layouts: 19.2 us -> 2.35 us
  between operations: 14.6 us -> 0.65 us
  other arithmetic: 10.1 us -> 0 us
    psum x3 -> x0, waiting for transfers between devices: 180 us -> none  [combine(): lax.psum((gate_part, up_part, grad_part), 'row')]
    all_gather x6 -> x0, blocking collectives: 140 us -> none  [the longest x3 72.5 us: shards(): lax.all_gather(local_input, 'col', axis=0, tiled=True)]
    pallas_call x0 -> x2, Pallas kernels: none -> 97.4 us  [the longest x1 90.7 us: relay_call(): pl.pallas_call(relay_kernel, name='relay', out_shape=(jax.ShapeDtypeStruc...]
    dot_general x24 -> x0, matrix products: 79.1 us -> none  [the longest x3 17.8 us: shards(): jnp.einsum('td,tf->df', rows_input, grad_up, preferred_element_type=jnp.f...]
    reduce_scatter x3 -> x0, waiting for transfers between devices: 48.8 us -> none  [shards(): lax.psum_scatter(partial_back, 'col', scatter_dimension=0, tiled=True)]
    reshape x6 -> x0, local copies, waits for them, and re-layouts: 8.65 us -> none  [shards(): keep_mask = jnp.broadcast_to(block_on[:, None, :, None], (block_count, TB...]
    convert_element_type x3 -> x0, other arithmetic: 6.45 us -> none  [activate(): (keep_mask * 2.0 * positive * up_total * grad_total).astype(jnp.bfloat16)]
  transfers between devices with their start and end apart: 8 -> 0, of which waited for: 7 -> 0; matrix products, arithmetic and copies ran while one was open for 14% -> 0% of each run, Pallas kernels for 0% -> 0%
where the time goes in v1:
time: 101 us; the launch traced here: 100 us
  Pallas kernels  97.4 us (96%)
  local copies, waits for them, and re-layouts  2.35 us (2%)
    pallas_call x1, Pallas kernels, relay_call(): pl.pallas_call(relay_kernel, name='relay', out_shape=(jax.ShapeDtypeStruc...  90.7 us
    pallas_call x1, Pallas kernels, weights_call(): pl.pallas_call(weights_kernel, name='weight_grads', grid=(FL // 256,), ou...  6.66 us
    unnamed x6, local copies, waits for them, and re-layouts  2.35 us

profile of v1, /device:TPU:1, one launch (start us, length us, event | category | flops | bytes accessed | tf_op | source)
XLA Modules:
  0.0 100.4 jit_solution(10974843252760239101)
XLA Ops:
  0.6 0.0 copy-start
  0.6 0.8 copy-done
  1.5 0.0 copy-start.1
  1.5 0.8 copy-done.1
  2.3 0.0 copy-start.2
  2.3 0.7 copy-done.2
  3.0 90.7 %relay.1 = (bf16[1,2,16,1024]{3,2,1,0:T(8,128)(2,1)S(1)}, bf16[2,128,1024]{2,1,0:T(8,128)(2,1)S(1)}, bf16[2,128,1024]{2,1,0:T(8,128)(2,1)S(1)}, bf16[2,128,1792]...) custom-call(bf16[1,2,16,1024]{3,2,1,0:T(8,128)(2,1)S(1)} %copy-done, ...), custom_call_target="tpu_custom_call" | custom-call | flops 5368709120 | bytes 16777216 | tf_op jit(solution)/shard_map/relay/pallas_call | solution.py:450
  93.7 6.7 %weight_grads.1 = (bf16[1,2,16,1024]{3,2,1,0:T(8,128)(2,1)}, bf16[1,1024,1792]{2,1,0:T(8,128)(2,1)}, bf16[1,1024,1792]{2,1,0:T(8,128)(2,1)}, bf16[1,1792,1024]{2,1,0:T(8,128)(2,1)}) custom-call(bf16[256,1024]{1,0:T(8,128)(2,1)S(1)} %bitcast.8, bf16[256,1024]{1,0:T(8,128)(2,1)S(1)} %bitcast.9, bf16[256,1792]{1,0:T(8,128)(2,1)S(1)} %bitcast.5, ...), custom_call_target="tpu_custom_call" | custom-call | tf_op jit(solution)/shard_map/weight_grads/pallas_call | solution.py:502
Async XLA Ops:
  0.6 0.8 copy-start
  1.5 0.8 copy-start.1
  2.3 0.7 copy-start.2

commit v2 on v0

v2 whole, which is shorter than its diff:
```python
import functools

import jax
import jax.numpy as jnp
from jax import lax
from jax.experimental import pallas as pl
from jax.experimental.pallas import tpu as pltpu
from jax.sharding import PartitionSpec as P

MESH = pl.DeviceIdType.MESH
F32, BF16 = jnp.float32, jnp.bfloat16
NT = (((1,), (1,)), ((), ()))
TN = (((0,), (0,)), ((), ()))

BLK = 64
TOK = 128
DL = 1024
FL = 1792
NBLK = 28
SLOTS = 14
HALF = 7
COL_STEPS = ((1, 0), (3, 0), (2, 0), (0, 1), (1, 1), (3, 1), (2, 1))


def relay_kernel(
    plans,
    x_hbm, top_hbm, wg_hbm, wu_hbm, wd_hbm, act_hbm,
    sent_hbm, xall_hbm, dyall_hbm, hid_hbm, gh_hbm, gu_hbm,
    xs, dys, wg, wu, wd, wgt, wut, wdt, dn, ps, pr, yo, ys, yr,
    agb0, agb1, agh0, agh1, hid, gh, gu, dxf, dxs, rr, sentv, act_ref, inv_y, inv_i,
    w_sem, own_sem, out_sem,
    x_s, x_r, dy_s, dy_r, pair_s, pair_r, y_s, y_r,
    ag_s, ag_r, agp_s, agp_r, hg_s, hg_r, hgp_s, hgp_r, rs_s, rs_r, hand_s, hand_r,
):
    agb, agh = (agb0, agb1), (agh0, agh1)
    sec, row, col = (lax.axis_index(a) for a in ("section", "row", "col"))
    y, k = row // 2, lax.rem(row, 2)
    z, xl = col // 2, lax.rem(col, 2)
    last = sec == 1

    def at_col(step, sign=1):
        dz, dx = step
        zz = lax.rem(z + (dz if sign > 0 else 4 - dz), 4)
        return zz * 2 + ((1 - xl) if dx else xl)

    def col_dev(step, sign=1):
        return (sec, row, at_col(step, sign))

    def y_at(d):
        return lax.rem(y + d, 4)

    def y_dev(d):
        return (sec, y_at(d) * 2 + k, col)

    pair = (sec, 2 * y + 1 - k, col)
    relay = (1 - sec, row, 2 * z + 1 - xl)

    def remote(src, dst, ss, rs, dev):
        return pltpu.make_async_remote_copy(
            src_ref=src, dst_ref=dst, send_sem=ss, recv_sem=rs, device_id=dev, device_id_type=MESH
        )

    def rows16(c):
        return pl.ds(pl.multiple_of(c * 16, 16), 16)

    lists = pltpu.make_async_copy(act_hbm, act_ref, own_sem.at[4])
    weights = [
        pltpu.make_async_copy(src.at[0], dst, w_sem.at[i])
        for i, (src, dst) in enumerate(((wg_hbm, wg), (wu_hbm, wu), (wd_hbm, wd)))
    ]
    own_x = [
        pltpu.make_async_copy(x_hbm.at[0, m], xs.at[m, rows16(col)], own_sem.at[m]) for m in range(2)
    ]
    own_dy = [
        pltpu.make_async_copy(top_hbm.at[m], dys.at[m, rows16(col)], own_sem.at[2 + m])
        for m in range(2)
    ]
    lists.start()
    for c in own_x:
        c.start()
    for c in weights:
        c.start()

    barrier = pltpu.get_barrier_semaphore()
    partners = [col_dev(s) for s in COL_STEPS] + [y_dev(d) for d in (1, 2, 3)] + [pair, relay]
    for dev in partners:
        pl.semaphore_signal(barrier, inc=1, device_id=dev, device_id_type=MESH)
    pl.semaphore_wait(barrier, len(partners))

    def invert():
        lists.wait()
        for m in range(2):
            agb[m][4] = jnp.zeros(agb[m].shape[1:], BF16)
            agh[m][4] = jnp.zeros(agh[m].shape[1:], BF16)
            for tb in range(2):
                def body(n, _):
                    slot = jnp.int32(2 * SLOTS)
                    for s in range(SLOTS):
                        slot = jnp.where(act_ref[0, m, tb, 0, s] == n, s, slot)
                    inv_y[m, tb, n] = jnp.where(slot < SLOTS, 2 * tb + jnp.where(slot < HALF, 0, 1), 4)
                    inv_i[m, tb, n] = jnp.where(
                        slot < SLOTS, jnp.where(slot < HALF, slot, slot - HALF), 0
                    )
                    return 0

                lax.fori_loop(0, NBLK, body, 0)

    left = lax.broadcasted_iota(jnp.int32, (32, 128), 1) < 64
    left16 = lax.broadcasted_iota(jnp.int32, (16, 128), 1) < 64
    MATS = ((0, 2), (2, 1))
    far_first = (6, 4, 5, 2, 3, 0, 1)

    def run(is_last, plan, expected):
        sends, recvs, local = {}, {}, {}

        def start(key, src, dst, ss, rs, dev, landing=None):
            c = remote(src, dst, ss, rs, dev)
            c.start()
            sends[key] = c
            if landing is not None:
                recvs[key] = remote(landing, landing, ss, rs, dev)

        def arrived(*key):
            recvs.pop(key).wait_recv()

        local.update({("w", i): c for i, c in enumerate(weights)})
        local.update({("x", m): c for m, c in enumerate(own_x)})

        def start_local(key, src, dst, sem):
            c = pltpu.make_async_copy(src, dst, sem)
            c.start()
            local[key] = c

        def dy_block(c):
            return c if is_last else c + 1 - 2 * lax.rem(c, 2)

        def lay_out(acc, m, mat, j):
            for tb in range(2):
                for h in range(2):
                    lo = acc[64 * tb : 64 * tb + 32, 128 * h : 128 * h + 128]
                    hi = acc[64 * tb + 32 : 64 * tb + 64, 128 * h : 128 * h + 128]
                    dn[m, mat, tb, 4 * j + 2 * h] = jnp.where(left, lo, pltpu.roll(hi, 64, 1))
                    dn[m, mat, tb, 4 * j + 2 * h + 1] = jnp.where(left, pltpu.roll(lo, 64, 1), hi)

        def send_pair(m, j):
            lo, n = MATS[j]
            far = pl.ds(pl.multiple_of(16 * (1 - k), 16), 16)

            def body(i, _):
                for yy in range(4):
                    tb, sh = yy // 2, yy % 2
                    b = jnp.minimum(act_ref[0, m, tb, 0, sh * HALF + i], NBLK - 1)
                    for mat in range(lo, lo + n):
                        ps[m, mat, yy, i] = dn[m, mat, tb, b, far, :]
                return 0

            lax.fori_loop(0, HALF, body, 0, unroll=True)
            cut = pl.ds(lo, n)
            start(
                ("pair", m, j), ps.at[m, cut], pr.at[m, cut], pair_s.at[m, j], pair_r.at[m, j], pair,
                pr.at[m, cut],
            )

        def spread_x(m):
            for i in far_first:
                step = COL_STEPS[i]
                start(
                    ("x", m, i), x_hbm.at[0, m], xs.at[m, rows16(col)], x_s.at[m, i], x_r.at[m, i],
                    col_dev(step), xs.at[m, rows16(at_col(step, -1))],
                )

        def spread_top(m):
            own_dy[m].start()
            local["dy", m] = own_dy[m]
            spread_dy(m, top_hbm.at[m])

        def wait_x(m):
            local.pop(("x", m)).wait()
            for i in range(7):
                arrived("x", m, i)

        def spread_dy(m, src):
            block = rows16(dy_block(col))
            for i in far_first:
                step = COL_STEPS[i]
                start(
                    ("dy", m, i), src, dys.at[m, block], dy_s.at[m, i], dy_r.at[m, i],
                    col_dev(step), dys.at[m, rows16(dy_block(at_col(step, -1)))],
                )

        def take_dy(m):
            arrived("hand", m)
            spread_dy(m, dys.at[m, rows16(dy_block(col))])

        def gate_up(m):
            if m == 0:
                local.pop(("w", 0)).wait()
                local.pop(("w", 1)).wait()
            start_local((0, m), xs.at[m], xall_hbm.at[m], out_sem.at[0, m])

            def body(j, _):
                cut = pl.ds(pl.multiple_of(j * 256, 256), 256)
                lay_out(jnp.dot(xs[m], wg[:, cut], preferred_element_type=F32), m, 0, j)
                lay_out(jnp.dot(xs[m], wu[:, cut], preferred_element_type=F32), m, 1, j)
                return 0

            lax.fori_loop(0, 7, body, 0, unroll=True)
            send_pair(m, 0)

        def back(m):
            if is_last:
                local.pop(("dy", m)).wait()
            if ("w", 2) in local:
                local.pop(("w", 2)).wait()
            for i in range(7):
                arrived("dy", m, i)
            start_local((1, m), dys.at[m], dyall_hbm.at[m], out_sem.at[1, m])

            def body(j, _):
                cut = pl.ds(pl.multiple_of(j * 256, 256), 256)
                if is_last:
                    grad = lax.dot_general(dys[m], wd[cut, :], NT, preferred_element_type=F32)
                else:
                    grad = jnp.dot(dys[m], wdt[:, cut], preferred_element_type=F32)
                lay_out(grad, m, 2, j)
                return 0

            lax.fori_loop(0, 7, body, 0, unroll=True)
            send_pair(m, 1)

        def reduce_pair(m, j):
            arrived("pair", m, j)
            lo, n = MATS[j]
            near = pl.ds(pl.multiple_of(16 * k, 16), 16)
            cut = pl.ds(lo, n)
            for d in (2, 1, 3, 0):
                yy = y_at(d)
                tb, sh = yy // 2, lax.rem(yy, 2)

                def body(i, _):
                    b = jnp.minimum(act_ref[0, m, tb, 0, sh * HALF + i], NBLK - 1)
                    for mat in range(lo, lo + n):
                        total = dn[m, mat, tb, b, near, :] + pr[m, mat, yy, i]
                        if d:
                            ys[m, d - 1, mat, i] = total.astype(BF16)
                        else:
                            yo[m, mat, i] = total
                    return 0

                lax.fori_loop(0, HALF, body, 0, unroll=True)
                if d:
                    start(
                        ("y", m, j, d), ys.at[m, d - 1, cut], yr.at[m, d - 1, cut],
                        y_s.at[m, j, d - 1], y_r.at[m, j, d - 1], y_dev(d), yr.at[m, d - 1, cut],
                    )

        def spread(name, buf, m, sems):
            ss, rs, pss, prs = sems
            for d in (2, 1, 3):
                start(
                    (name, m, d), buf.at[y, k], buf.at[y, k], ss.at[m, d - 1], rs.at[m, d - 1], y_dev(d),
                    buf.at[y_at(4 - d), k],
                )
            start((name + "p", m, 0), buf.at[y, k], buf.at[y, k], pss.at[m, 0], prs.at[m, 0], pair, buf.at[y, 1 - k])

        def forward(name, buf, m, sems):
            ss, rs, pss, prs = sems
            for d in (1, 3, 2):
                arrived(name, m, d)
                yy = y_at(4 - d)
                start(
                    (name + "p", m, d), buf.at[yy, k], buf.at[yy, k], pss.at[m, d], prs.at[m, d], pair,
                    buf.at[yy, 1 - k],
                )

        grad_sems, hid_sems = (ag_s, ag_r, agp_s, agp_r), (hg_s, hg_r, hgp_s, hgp_r)

        def activate(m):
            for j in range(2):
                for d in (1, 2, 3):
                    arrived("y", m, j, d)

            def body(i, _):
                sums = []
                for mat in range(3):
                    total = yo[m, mat, i]
                    for d in range(3):
                        total = total + yr[m, d, mat, i].astype(F32)
                    sums.append(total)
                gate, up, grad = sums
                r = jnp.maximum(gate, 0.0)
                sq = r * r
                agh[m][y, k, i] = (sq * up).astype(BF16)
                agb[m][y, k, 0, i] = (2.0 * r * up * grad).astype(BF16)
                agb[m][y, k, 1, i] = (sq * grad).astype(BF16)
                return 0

            lax.fori_loop(0, HALF, body, 0, unroll=True)
            spread("g", agb[m], m, grad_sems)
            spread("h", agh[m], m, hid_sems)

        def forward_grads(m):
            forward("g", agb[m], m, grad_sems)

        def expand(m, sources, targets):
            def body(n, _):
                cut = pl.ds(pl.multiple_of(n * 128, 128), 128)
                for tb in range(2):
                    ya, ia = inv_y[m, tb, 2 * n], inv_i[m, tb, 2 * n]
                    yb, ib = inv_y[m, tb, 2 * n + 1], inv_i[m, tb, 2 * n + 1]
                    for kk in range(2):
                        for src, dst in zip(sources, targets):
                            a = src(ya, kk, ia).astype(F32)
                            b = src(yb, kk, ib).astype(F32)
                            top = 64 * tb + 16 * kk
                            dst[m, top : top + 16, cut] = jnp.where(left16, a, pltpu.roll(b, 64, 1)).astype(BF16)
                            dst[m, top + 32 : top + 48, cut] = jnp.where(left16, pltpu.roll(a, 64, 1), b).astype(BF16)
                return 0

            lax.fori_loop(0, NBLK // 2, body, 0, unroll=True)

        def expand_grads(m):
            for d in (0, 1, 3, 2):
                arrived("gp", m, d)
            expand(
                m, (lambda a, b, c: agb[m][a, b, 0, c], lambda a, b, c: agb[m][a, b, 1, c]), (gh, gu)
            )
            start_local((3, m), gh.at[m], gh_hbm.at[m], out_sem.at[3, m])
            start_local((4, m), gu.at[m], gu_hbm.at[m], out_sem.at[4, m])

        def input_grad(m):
            def body(j, half):
                cut = pl.ds(pl.multiple_of(j * 256, 256), 256)
                rows = pl.ds(pl.multiple_of(half * 512 + j * 256, 256), 256)
                if is_last:
                    part = lax.dot_general(gh[m], wg[rows, :], NT, preferred_element_type=F32)
                    part = part + lax.dot_general(gu[m], wu[rows, :], NT, preferred_element_type=F32)
                else:
                    part = jnp.dot(gh[m], wgt[:, rows], preferred_element_type=F32)
                    part = part + jnp.dot(gu[m], wut[:, rows], preferred_element_type=F32)
                dxf[m, half, :, cut] = part
                dxs[m, half, :, cut] = part.astype(BF16)

            for half in range(2):
                lax.fori_loop(0, 2, lambda j, c: (body(j, half), c)[1], 0, unroll=True)
                for i in far_first:
                    start(
                        ("rs", m, half, i), dxs.at[m, half, rows16(at_col(COL_STEPS[i]))], rr.at[m, half, i],
                        rs_s.at[m, half, i], rs_r.at[m, half, i], col_dev(COL_STEPS[i]), rr.at[m, half, i],
                    )

        def finish(m):
            for half in range(2):
                cols = slice(512 * half, 512 * half + 512)
                for i in range(7):
                    arrived("rs", m, half, i)
                total = dys[m, rows16(col), cols].astype(F32) + dxf[m, half, rows16(col), :]
                for i in range(7):
                    total = total + rr[m, half, i].astype(F32)
                sentv[m, :, cols] = total.astype(BF16)
            if is_last:
                start(("hand", m), sentv.at[m], dys.at[m, rows16(col)], hand_s.at[m], hand_r.at[m], relay)
            start_local((5, m), sentv.at[m], sent_hbm.at[0, m], out_sem.at[5, m])

        def turn():
            for i in range(3):
                if ("w", i) in local:
                    local.pop(("w", i)).wait()

            def body(j, _):
                cut = pl.ds(pl.multiple_of(j * 256, 256), 256)
                wgt[cut, :] = wg[:, cut].T
                wut[cut, :] = wu[:, cut].T
                wdt[:, cut] = wd[cut, :].T
                return 0

            lax.fori_loop(0, 7, body, 0)

        def hidden(m):
            forward("h", agh[m], m, hid_sems)
            for d in range(4):
                arrived("hp", m, d)
            expand(m, (lambda a, b, c: agh[m][a, b, c],), (hid,))
            start_local((2, m), hid.at[m], hid_hbm.at[m], out_sem.at[2, m])

        for m in expected:
            block = dys.at[m, rows16(dy_block(col))]
            recvs["hand", m] = remote(block, block, hand_s.at[m], hand_r.at[m], relay)
        table = dict(
            ax=spread_x, ady=spread_top, wx=wait_x, inv=invert, turn=turn, gu=gate_up, bk=back, rp=reduce_pair, act=activate, fwd=forward_grads, ex=expand_grads,
            dx=input_grad, fin=finish, hid=hidden, dy=take_dy,
        )
        for name, *where in plan:
            table[name](*where)
        for c in sends.values():
            c.wait_send()
        for c in recvs.values():
            c.wait_recv()
        for c in local.values():
            c.wait()

    plan0, plan1 = plans
    handed = tuple(m for m in range(2) if ("fin", m) in plan1)

    @pl.when(last)
    def _():
        run(True, plan1, ())

    @pl.when(sec == 0)
    def _():
        run(False, plan0, handed)


PLAN1 = (
    ("ax", 0), ("ady", 0), ("inv",), ("wx", 0), ("ax", 1), ("ady", 1), ("gu", 0), ("bk", 0), ("rp", 0, 0), ("rp", 0, 1),
    ("wx", 1), ("gu", 1), ("bk", 1), ("act", 0), ("rp", 1, 0), ("rp", 1, 1), ("fwd", 0), ("ex", 0), ("dx", 0), ("act", 1),
    ("fin", 0), ("fwd", 1), ("ex", 1), ("dx", 1), ("hid", 0), ("fin", 1), ("hid", 1),
)
PLAN0 = (
    ("ax", 0), ("ax", 1), ("inv",), ("wx", 0), ("gu", 0), ("wx", 1), ("gu", 1), ("rp", 0, 0), ("rp", 1, 0), ("turn",),
    ("dy", 0), ("bk", 0), ("rp", 0, 1), ("dy", 1), ("act", 0), ("bk", 1), ("fwd", 0), ("rp", 1, 1), ("ex", 0), ("dx", 0),
    ("act", 1), ("hid", 0), ("fwd", 1), ("ex", 1), ("dx", 1), ("hid", 1), ("fin", 0), ("fin", 1),
)


def relay_call(layer_input, top_grad, gate_weight, up_weight, down_weight, activity, plans=(PLAN0, PLAN1), number=1):
    any_space = pl.BlockSpec(memory_space=pl.ANY)
    hbm = pl.BlockSpec(memory_space=pltpu.HBM)
    dma = pltpu.SemaphoreType.DMA
    vm = pltpu.VMEM
    tile = (HALF, 16, 128)
    return pl.pallas_call(
        functools.partial(relay_kernel, plans),
        name="relay",
        out_shape=(
            jax.ShapeDtypeStruct((1, 2, 16, DL), BF16),
            jax.ShapeDtypeStruct((2, TOK, DL), BF16),
            jax.ShapeDtypeStruct((2, TOK, DL), BF16),
            jax.ShapeDtypeStruct((2, TOK, FL), BF16),
            jax.ShapeDtypeStruct((2, TOK, FL), BF16),
            jax.ShapeDtypeStruct((2, TOK, FL), BF16),
        ),
        in_specs=[hbm] * 6,
        out_specs=(any_space,) * 6,
        scratch_shapes=[
            vm((2, TOK, DL), BF16), vm((2, TOK, DL), BF16),
            vm((DL, FL), BF16), vm((DL, FL), BF16), vm((FL, DL), BF16),
            vm((FL, DL), BF16), vm((FL, DL), BF16), vm((DL, FL), BF16),
            vm((2, 3, 2, NBLK, 32, 128), F32),
            vm((2, 3, 4) + tile, F32), vm((2, 3, 4) + tile, F32),
            vm((2, 3) + tile, F32), vm((2, 3, 3) + tile, BF16), vm((2, 3, 3) + tile, BF16),
            vm((5, 2, 2) + tile, BF16), vm((5, 2, 2) + tile, BF16),
            vm((5, 2) + tile, BF16), vm((5, 2) + tile, BF16),
            vm((2, TOK, FL), BF16), vm((2, TOK, FL), BF16), vm((2, TOK, FL), BF16),
            vm((2, 2, TOK, DL // 2), F32), vm((2, 2, TOK, DL // 2), BF16), vm((2, 2, 7, 16, DL // 2), BF16),
            vm((2, 16, DL), BF16),
            pltpu.SMEM((1, 2, 2, 1, SLOTS), jnp.int32),
            pltpu.SMEM((2, 2, NBLK), jnp.int32), pltpu.SMEM((2, 2, NBLK), jnp.int32),
            dma((3,)), dma((5,)), dma((6, 2)),
            dma((2, 7)), dma((2, 7)), dma((2, 7)), dma((2, 7)),
            dma((2, 2)), dma((2, 2)), dma((2, 2, 3)), dma((2, 2, 3)),
            dma((2, 3)), dma((2, 3)), dma((2, 4)), dma((2, 4)),
            dma((2, 3)), dma((2, 3)), dma((2, 4)), dma((2, 4)),
            dma((2, 2, 7)), dma((2, 2, 7)), dma((2,)), dma((2,)),
        ],
        compiler_params=pltpu.CompilerParams(
            collective_id=number, has_side_effects=True, vmem_limit_bytes=48 * 2**20
        ),
        cost_estimate=pl.CostEstimate(flops=5 * 2**30, bytes_accessed=16 * 2**20, transcendentals=0),
    )(*(
        pltpu.with_memory_space_constraint(a, pltpu.HBM)
        for a in (layer_input, top_grad, gate_weight, up_weight, down_weight, activity)
    ))


def weights_kernel(x_ref, dy_ref, hid_ref, gh_ref, gu_ref, sent_ref, out_sent, og, ou, od, xt):
    @pl.when(pl.program_id(0) == 0)
    def _():
        xt[...] = x_ref[...].T
        out_sent[...] = sent_ref[...]

    og[0] = jnp.dot(xt[...], gh_ref[...], preferred_element_type=F32).astype(BF16)
    ou[0] = jnp.dot(xt[...], gu_ref[...], preferred_element_type=F32).astype(BF16)
    od[0] = lax.dot_general(hid_ref[...], dy_ref[...], TN, preferred_element_type=F32).astype(BF16)


def weights_call(x_all, dy_all, hid, gh, gu, sent):
    whole = lambda shape: pl.BlockSpec(shape, lambda j: (0,) * len(shape))
    cut = pl.BlockSpec((2 * TOK, 256), lambda j: (0, j))
    return pl.pallas_call(
        weights_kernel,
        name="weight_grads",
        grid=(FL // 256,),
        out_shape=(
            jax.ShapeDtypeStruct((1, 2, 16, DL), BF16),
            jax.ShapeDtypeStruct((1, DL, FL), BF16),
            jax.ShapeDtypeStruct((1, DL, FL), BF16),
            jax.ShapeDtypeStruct((1, FL, DL), BF16),
        ),
        in_specs=[whole((2 * TOK, DL)), whole((2 * TOK, DL)), cut, cut, cut, whole((1, 2, 16, DL))],
        out_specs=(
            whole((1, 2, 16, DL)),
            pl.BlockSpec((1, DL, 256), lambda j: (0, 0, j)),
            pl.BlockSpec((1, DL, 256), lambda j: (0, 0, j)),
            pl.BlockSpec((1, 256, DL), lambda j: (0, j, 0)),
        ),
        scratch_shapes=[pltpu.VMEM((DL, 2 * TOK), BF16)],
        compiler_params=pltpu.CompilerParams(
            dimension_semantics=("arbitrary",), vmem_limit_bytes=24 * 2**20
        ),
    )(x_all, dy_all, hid, gh, gu, sent)


def shards(layer_input, top_grad, gate_weight, up_weight, down_weight, activity):
    sent, x_all, dy_all, hid, gh, gu = relay_call(
        layer_input, top_grad, gate_weight, up_weight, down_weight, activity
    )
    flat = lambda a: a.reshape(2 * TOK, a.shape[-1])
    return weights_call(flat(x_all), flat(dy_all), flat(hid), flat(gh), flat(gu), sent)


def solution(mesh):
    in_specs = (
        P("section", None, "col", "row"),
        P(None, "col", "row"),
        P("section", "row", "col"),
        P("section", "row", "col"),
        P("section", "col", "row"),
        P("section", None, None, "col", None),
    )
    out_specs = (
        P("section", None, "col", "row"),
        P("section", "row", "col"),
        P("section", "row", "col"),
        P("section", "col", "row"),
    )
    return jax.shard_map(shards, mesh=mesh, in_specs=in_specs, out_specs=out_specs, check_vma=False)
```

time: 501 us -> 85.5 us (0.17)
  waiting for transfers between devices: 230 us -> 0 us
  blocking collectives: 140 us -> 0 us
  Pallas kernels: 0 us -> 84.7 us
  matrix products: 79.1 us -> 0 us
  local copies, waits for them, and re-layouts: 19.2 us -> 0 us
  between operations: 14.6 us -> 0.64 us
  other arithmetic: 10.1 us -> 0 us
    psum x3 -> x0, waiting for transfers between devices: 180 us -> none  [combine(): lax.psum((gate_part, up_part, grad_part), 'row')]
    all_gather x6 -> x0, blocking collectives: 140 us -> none  [the longest x3 72.5 us: shards(): lax.all_gather(local_input, 'col', axis=0, tiled=True)]
    pallas_call x0 -> x2, Pallas kernels: none -> 84.7 us  [the longest x1 78.1 us: relay_call(): pl.pallas_call(functools.partial(relay_kernel, plans), name='relay', out_...]
    dot_general x24 -> x0, matrix products: 79.1 us -> none  [the longest x3 17.8 us: shards(): jnp.einsum('td,tf->df', rows_input, grad_up, preferred_element_type=jnp.f...]
    reduce_scatter x3 -> x0, waiting for transfers between devices: 48.8 us -> none  [shards(): lax.psum_scatter(partial_back, 'col', scatter_dimension=0, tiled=True)]
    reshape x6 -> x0, local copies, waits for them, and re-layouts: 8.65 us -> none  [shards(): keep_mask = jnp.broadcast_to(block_on[:, None, :, None], (block_count, TB...]
    convert_element_type x3 -> x0, other arithmetic: 6.45 us -> none  [activate(): (keep_mask * 2.0 * positive * up_total * grad_total).astype(jnp.bfloat16)]
  transfers between devices with their start and end apart: 8 -> 0, of which waited for: 7 -> 0; matrix products, arithmetic and copies ran while one was open for 14% -> 0% of each run, Pallas kernels for 0% -> 0%
where the time goes in v2:
time: 85.5 us; the launch traced here: 85.4 us
  Pallas kernels  84.7 us (99%)
    pallas_call x1, Pallas kernels, relay_call(): pl.pallas_call(functools.partial(relay_kernel, plans), name='relay', out_...  78.1 us
    pallas_call x1, Pallas kernels, weights_call(): pl.pallas_call(weights_kernel, name='weight_grads', grid=(FL // 256,), ou...  6.65 us

profile of v2, /device:TPU:1, one launch (start us, length us, event | category | flops | bytes accessed | tf_op | source)
XLA Modules:
  0.0 85.4 jit_solution(15904543251289228101)
XLA Ops:
  0.6 78.1 %relay.1 = (bf16[1,2,16,1024]{3,2,1,0:T(8,128)(2,1)S(1)}, bf16[2,128,1024]{2,1,0:T(8,128)(2,1)S(1)}, bf16[2,128,1024]{2,1,0:T(8,128)(2,1)S(1)}, bf16[2,128,1792]...) custom-call(bf16[1,2,16,1024]{3,2,1,0:T(8,128)(2,1)} %x_hbm.1, ...), custom_call_target="tpu_custom_call" | custom-call | flops 5368709120 | bytes 16777216 | tf_op jit(solution)/shard_map/relay/pallas_call | solution.py:432
  78.7 6.7 %weight_grads.1 = (bf16[1,2,16,1024]{3,2,1,0:T(8,128)(2,1)}, bf16[1,1024,1792]{2,1,0:T(8,128)(2,1)}, bf16[1,1024,1792]{2,1,0:T(8,128)(2,1)}, bf16[1,1792,1024]{2,1,0:T(8,128)(2,1)}) custom-call(bf16[256,1024]{1,0:T(8,128)(2,1)S(1)} %bitcast.8, bf16[256,1024]{1,0:T(8,128)(2,1)S(1)} %bitcast.9, bf16[256,1792]{1,0:T(8,128)(2,1)S(1)} %bitcast.5, ...), custom_call_target="tpu_custom_call" | custom-call | tf_op jit(solution)/shard_map/weight_grads/pallas_call | solution.py:490

commit v3 on v2

--- a/solution.py
+++ b/solution.py
@@ -25,8 +25,8 @@
 def relay_kernel(
     plans,
     x_hbm, top_hbm, wg_hbm, wu_hbm, wd_hbm, act_hbm,
-    sent_hbm, xall_hbm, dyall_hbm, hid_hbm, gh_hbm, gu_hbm,
-    xs, dys, wg, wu, wd, wgt, wut, wdt, dn, ps, pr, yo, ys, yr,
+    sent_hbm, xt_hbm, dyall_hbm, hid_hbm, gh_hbm, gu_hbm,
+    xs, xt, dys, wg, wu, wd, wgt, wut, wdt, dn, ps, pr, yo, ys, yr,
     agb0, agb1, agh0, agh1, hid, gh, gu, dxf, dxs, rr, sentv, act_ref, inv_y, inv_i,
     w_sem, own_sem, out_sem,
     x_s, x_r, dy_s, dy_r, pair_s, pair_r, y_s, y_r,
@@ -109,6 +109,7 @@
     left16 = lax.broadcasted_iota(jnp.int32, (16, 128), 1) < 64
     MATS = ((0, 2), (2, 1))
     far_first = (6, 4, 5, 2, 3, 0, 1)
+    halves = (pl.ds(0, DL // 2), pl.ds(DL // 2, DL // 2))
 
     def run(is_last, plan, expected):
         sends, recvs, local = {}, {}, {}
@@ -172,32 +173,30 @@
         def spread_top(m):
             own_dy[m].start()
             local["dy", m] = own_dy[m]
-            spread_dy(m, top_hbm.at[m])
+            for half in range(2):
+                spread_dy(m, half, top_hbm.at[m, :, halves[half]])
 
         def wait_x(m):
             local.pop(("x", m)).wait()
             for i in range(7):
                 arrived("x", m, i)
 
-        def spread_dy(m, src):
+        def spread_dy(m, half, src):
             block = rows16(dy_block(col))
+            cols = halves[half]
             for i in far_first:
                 step = COL_STEPS[i]
                 start(
-                    ("dy", m, i), src, dys.at[m, block], dy_s.at[m, i], dy_r.at[m, i],
-                    col_dev(step), dys.at[m, rows16(dy_block(at_col(step, -1)))],
+                    ("dy", m, half, i), src, dys.at[m, block, cols], dy_s.at[m, half, i], dy_r.at[m, half, i],
+                    col_dev(step), dys.at[m, rows16(dy_block(at_col(step, -1))), cols],
                 )
 
         def take_dy(m):
-            arrived("hand", m)
-            spread_dy(m, dys.at[m, rows16(dy_block(col))])
+            for half in range(2):
+                arrived("hand", m, half)
+                spread_dy(m, half, dys.at[m, rows16(dy_block(col)), halves[half]])
 
         def gate_up(m):
-            if m == 0:
-                local.pop(("w", 0)).wait()
-                local.pop(("w", 1)).wait()
-            start_local((0, m), xs.at[m], xall_hbm.at[m], out_sem.at[0, m])
-
             def body(j, _):
                 cut = pl.ds(pl.multiple_of(j * 256, 256), 256)
                 lay_out(jnp.dot(xs[m], wg[:, cut], preferred_element_type=F32), m, 0, j)
@@ -210,18 +209,14 @@
         def back(m):
             if is_last:
                 local.pop(("dy", m)).wait()
-            if ("w", 2) in local:
-                local.pop(("w", 2)).wait()
-            for i in range(7):
-                arrived("dy", m, i)
+            for half in range(2):
+                for i in range(7):
+                    arrived("dy", m, half, i)
             start_local((1, m), dys.at[m], dyall_hbm.at[m], out_sem.at[1, m])
 
             def body(j, _):
                 cut = pl.ds(pl.multiple_of(j * 256, 256), 256)
-                if is_last:
-                    grad = lax.dot_general(dys[m], wd[cut, :], NT, preferred_element_type=F32)
-                else:
-                    grad = jnp.dot(dys[m], wdt[:, cut], preferred_element_type=F32)
+                grad = jnp.dot(dys[m], wdt[:, cut], preferred_element_type=F32)
                 lay_out(grad, m, 2, j)
                 return 0
 
@@ -275,28 +270,40 @@
 
         grad_sems, hid_sems = (ag_s, ag_r, agp_s, agp_r), (hg_s, hg_r, hgp_s, hgp_r)
 
+        def total(m, mat, i):
+            value = yo[m, mat, i]
+            for d in range(3):
+                value = value + yr[m, d, mat, i].astype(F32)
+            return value
+
+        def gate_sums(m):
+            for d in (1, 2, 3):
+                arrived("y", m, 0, d)
+
+            def body(i, _):
+                r = jnp.maximum(total(m, 0, i), 0.0)
+                up = total(m, 1, i)
+                yo[m, 0, i] = r
+                yo[m, 1, i] = up
+                agh[m][y, k, i] = (r * r * up).astype(BF16)
+                return 0
+
+            lax.fori_loop(0, HALF, body, 0, unroll=True)
+
         def activate(m):
-            for j in range(2):
-                for d in (1, 2, 3):
-                    arrived("y", m, j, d)
+            for d in (1, 2, 3):
+                arrived("y", m, 1, d)
 
             def body(i, _):
-                sums = []
-                for mat in range(3):
-                    total = yo[m, mat, i]
-                    for d in range(3):
-                        total = total + yr[m, d, mat, i].astype(F32)
-                    sums.append(total)
-                gate, up, grad = sums
-                r = jnp.maximum(gate, 0.0)
-                sq = r * r
-                agh[m][y, k, i] = (sq * up).astype(BF16)
+                r, up, grad = yo[m, 0, i], yo[m, 1, i], total(m, 2, i)
                 agb[m][y, k, 0, i] = (2.0 * r * up * grad).astype(BF16)
-                agb[m][y, k, 1, i] = (sq * grad).astype(BF16)
+                agb[m][y, k, 1, i] = (r * r * grad).astype(BF16)
                 return 0
 
             lax.fori_loop(0, HALF, body, 0, unroll=True)
             spread("g", agb[m], m, grad_sems)
+
+        def spread_hidden(m):
             spread("h", agh[m], m, hid_sems)
 
         def forward_grads(m):
@@ -332,12 +339,8 @@
             def body(j, half):
                 cut = pl.ds(pl.multiple_of(j * 256, 256), 256)
                 rows = pl.ds(pl.multiple_of(half * 512 + j * 256, 256), 256)
-                if is_last:
-                    part = lax.dot_general(gh[m], wg[rows, :], NT, preferred_element_type=F32)
-                    part = part + lax.dot_general(gu[m], wu[rows, :], NT, preferred_element_type=F32)
-                else:
-                    part = jnp.dot(gh[m], wgt[:, rows], preferred_element_type=F32)
-                    part = part + jnp.dot(gu[m], wut[:, rows], preferred_element_type=F32)
+                part = jnp.dot(gh[m], wgt[:, rows], preferred_element_type=F32)
+                part = part + jnp.dot(gu[m], wut[:, rows], preferred_element_type=F32)
                 dxf[m, half, :, cut] = part
                 dxs[m, half, :, cut] = part.astype(BF16)
 
@@ -358,23 +361,36 @@
                 for i in range(7):
                     total = total + rr[m, half, i].astype(F32)
                 sentv[m, :, cols] = total.astype(BF16)
-            if is_last:
-                start(("hand", m), sentv.at[m], dys.at[m, rows16(col)], hand_s.at[m], hand_r.at[m], relay)
+                if is_last:
+                    start(
+                        ("hand", m, half), sentv.at[m, :, halves[half]], dys.at[m, rows16(col), halves[half]],
+                        hand_s.at[m, half], hand_r.at[m, half], relay,
+                    )
             start_local((5, m), sentv.at[m], sent_hbm.at[0, m], out_sem.at[5, m])
 
         def turn():
-            for i in range(3):
-                if ("w", i) in local:
-                    local.pop(("w", i)).wait()
+            for i, (src, dst) in enumerate(((wg, wgt), (wu, wut))):
+                local.pop(("w", i)).wait()
+
+                def body(j, _):
+                    cut = pl.ds(pl.multiple_of(j * 256, 256), 256)
+                    dst[cut, :] = src[:, cut].T
+                    return 0
+
+                lax.fori_loop(0, 7, body, 0)
+            local.pop(("w", 2)).wait()
 
             def body(j, _):
                 cut = pl.ds(pl.multiple_of(j * 256, 256), 256)
-                wgt[cut, :] = wg[:, cut].T
-                wut[cut, :] = wu[:, cut].T
                 wdt[:, cut] = wd[cut, :].T
                 return 0
 
             lax.fori_loop(0, 7, body, 0)
+
+        def turn_x():
+            for m in range(2):
+                xt[:, TOK * m : TOK * m + TOK] = xs[m].T
+            start_local((0, 0), xt, xt_hbm, out_sem.at[0, 0])
 
         def hidden(m):
             forward("h", agh[m], m, hid_sems)
@@ -384,10 +400,11 @@
             start_local((2, m), hid.at[m], hid_hbm.at[m], out_sem.at[2, m])
 
         for m in expected:
-            block = dys.at[m, rows16(dy_block(col))]
-            recvs["hand", m] = remote(block, block, hand_s.at[m], hand_r.at[m], relay)
+            for half in range(2):
+                block = dys.at[m, rows16(dy_block(col)), halves[half]]
+                recvs["hand", m, half] = remote(block, block, hand_s.at[m, half], hand_r.at[m, half], relay)
         table = dict(
-            ax=spread_x, ady=spread_top, wx=wait_x, inv=invert, turn=turn, gu=gate_up, bk=back, rp=reduce_pair, act=activate, fwd=forward_grads, ex=expand_grads,
+            ax=spread_x, ady=spread_top, wx=wait_x, inv=invert, turn=turn, gu=gate_up, gs=gate_sums, hs=spread_hidden, xt=turn_x, bk=back, rp=reduce_pair, act=activate, fwd=forward_grads, ex=expand_grads,
             dx=input_grad, fin=finish, hid=hidden, dy=take_dy,
         )
         for name, *where in plan:
@@ -412,14 +429,16 @@
 
 
 PLAN1 = (
-    ("ax", 0), ("ady", 0), ("inv",), ("wx", 0), ("ax", 1), ("ady", 1), ("gu", 0), ("bk", 0), ("rp", 0, 0), ("rp", 0, 1),
-    ("wx", 1), ("gu", 1), ("bk", 1), ("act", 0), ("rp", 1, 0), ("rp", 1, 1), ("fwd", 0), ("ex", 0), ("dx", 0), ("act", 1),
-    ("fin", 0), ("fwd", 1), ("ex", 1), ("dx", 1), ("hid", 0), ("fin", 1), ("hid", 1),
+    ("ax", 0), ("inv",), ("ady", 0), ("turn",), ("wx", 0), ("ax", 1), ("ady", 1), ("gu", 0), ("bk", 0), ("rp", 0, 0),
+    ("rp", 0, 1), ("wx", 1), ("gu", 1), ("gs", 0), ("rp", 1, 0), ("bk", 1), ("act", 0), ("rp", 1, 1), ("fwd", 0),
+    ("ex", 0), ("gs", 1), ("act", 1), ("dx", 0), ("fwd", 1), ("ex", 1), ("fin", 0), ("dx", 1), ("fin", 1),
+    ("hs", 0), ("hs", 1), ("xt",), ("hid", 0), ("hid", 1),
 )
 PLAN0 = (
-    ("ax", 0), ("ax", 1), ("inv",), ("wx", 0), ("gu", 0), ("wx", 1), ("gu", 1), ("rp", 0, 0), ("rp", 1, 0), ("turn",),
-    ("dy", 0), ("bk", 0), ("rp", 0, 1), ("dy", 1), ("act", 0), ("bk", 1), ("fwd", 0), ("rp", 1, 1), ("ex", 0), ("dx", 0),
-    ("act", 1), ("hid", 0), ("fwd", 1), ("ex", 1), ("dx", 1), ("hid", 1), ("fin", 0), ("fin", 1),
+    ("ax", 0), ("ax", 1), ("inv",), ("turn",), ("wx", 0), ("gu", 0), ("wx", 1), ("gu", 1), ("rp", 0, 0), ("rp", 1, 0),
+    ("gs", 0), ("hs", 0), ("gs", 1), ("hs", 1), ("xt",), ("hid", 0), ("hid", 1), ("dy", 0), ("bk", 0), ("rp", 0, 1),
+    ("dy", 1), ("act", 0), ("bk", 1), ("rp", 1, 1), ("fwd", 0), ("ex", 0), ("act", 1), ("dx", 0), ("fwd", 1),
+    ("ex", 1), ("fin", 0), ("dx", 1), ("fin", 1),
 )
 
 
@@ -434,7 +453,7 @@
         name="relay",
         out_shape=(
             jax.ShapeDtypeStruct((1, 2, 16, DL), BF16),
-            jax.ShapeDtypeStruct((2, TOK, DL), BF16),
+            jax.ShapeDtypeStruct((DL, 2 * TOK), BF16),
             jax.ShapeDtypeStruct((2, TOK, DL), BF16),
             jax.ShapeDtypeStruct((2, TOK, FL), BF16),
             jax.ShapeDtypeStruct((2, TOK, FL), BF16),
@@ -443,7 +462,7 @@
         in_specs=[hbm] * 6,
         out_specs=(any_space,) * 6,
         scratch_shapes=[
-            vm((2, TOK, DL), BF16), vm((2, TOK, DL), BF16),
+            vm((2, TOK, DL), BF16), vm((DL, 2 * TOK), BF16), vm((2, TOK, DL), BF16),
             vm((DL, FL), BF16), vm((DL, FL), BF16), vm((FL, DL), BF16),
             vm((FL, DL), BF16), vm((FL, DL), BF16), vm((DL, FL), BF16),
             vm((2, 3, 2, NBLK, 32, 128), F32),
@@ -457,11 +476,11 @@
             pltpu.SMEM((1, 2, 2, 1, SLOTS), jnp.int32),
             pltpu.SMEM((2, 2, NBLK), jnp.int32), pltpu.SMEM((2, 2, NBLK), jnp.int32),
             dma((3,)), dma((5,)), dma((6, 2)),
-            dma((2, 7)), dma((2, 7)), dma((2, 7)), dma((2, 7)),
+            dma((2, 7)), dma((2, 7)), dma((2, 2, 7)), dma((2, 2, 7)),
             dma((2, 2)), dma((2, 2)), dma((2, 2, 3)), dma((2, 2, 3)),
             dma((2, 3)), dma((2, 3)), dma((2, 4)), dma((2, 4)),
             dma((2, 3)), dma((2, 3)), dma((2, 4)), dma((2, 4)),
-            dma((2, 2, 7)), dma((2, 2, 7)), dma((2,)), dma((2,)),
+            dma((2, 2, 7)), dma((2, 2, 7)), dma((2, 2)), dma((2, 2)),
         ],
         compiler_params=pltpu.CompilerParams(
             collective_id=number, has_side_effects=True, vmem_limit_bytes=48 * 2**20
@@ -473,20 +492,19 @@
     ))
 
 
-def weights_kernel(x_ref, dy_ref, hid_ref, gh_ref, gu_ref, sent_ref, out_sent, og, ou, od, xt):
+def weights_kernel(xt_ref, dy_ref, hid_ref, gh_ref, gu_ref, sent_ref, out_sent, og, ou, od):
     @pl.when(pl.program_id(0) == 0)
     def _():
-        xt[...] = x_ref[...].T
         out_sent[...] = sent_ref[...]
 
-    og[0] = jnp.dot(xt[...], gh_ref[...], preferred_element_type=F32).astype(BF16)
-    ou[0] = jnp.dot(xt[...], gu_ref[...], preferred_element_type=F32).astype(BF16)
-    od[0] = lax.dot_general(hid_ref[...], dy_ref[...], TN, preferred_element_type=F32).astype(BF16)
-
-
-def weights_call(x_all, dy_all, hid, gh, gu, sent):
+    cut = pl.ds(pl.multiple_of(pl.program_id(0) * 256, 256), 256)
+    og[0] = jnp.dot(xt_ref[...], gh_ref[:, cut], preferred_element_type=F32).astype(BF16)
+    ou[0] = jnp.dot(xt_ref[...], gu_ref[:, cut], preferred_element_type=F32).astype(BF16)
+    od[0] = lax.dot_general(hid_ref[:, cut], dy_ref[...], TN, preferred_element_type=F32).astype(BF16)
+
+
+def weights_call(xt, dy_all, hid, gh, gu, sent):
     whole = lambda shape: pl.BlockSpec(shape, lambda j: (0,) * len(shape))
-    cut = pl.BlockSpec((2 * TOK, 256), lambda j: (0, j))
     return pl.pallas_call(
         weights_kernel,
         name="weight_grads",
@@ -497,26 +515,25 @@
             jax.ShapeDtypeStruct((1, DL, FL), BF16),
             jax.ShapeDtypeStruct((1, FL, DL), BF16),
         ),
-        in_specs=[whole((2 * TOK, DL)), whole((2 * TOK, DL)), cut, cut, cut, whole((1, 2, 16, DL))],
+        in_specs=[pl.BlockSpec(memory_space=pltpu.VMEM)] * 6,
         out_specs=(
             whole((1, 2, 16, DL)),
             pl.BlockSpec((1, DL, 256), lambda j: (0, 0, j)),
             pl.BlockSpec((1, DL, 256), lambda j: (0, 0, j)),
             pl.BlockSpec((1, 256, DL), lambda j: (0, j, 0)),
         ),
-        scratch_shapes=[pltpu.VMEM((DL, 2 * TOK), BF16)],
         compiler_params=pltpu.CompilerParams(
             dimension_semantics=("arbitrary",), vmem_limit_bytes=24 * 2**20
         ),
-    )(x_all, dy_all, hid, gh, gu, sent)
+    )(xt, dy_all, hid, gh, gu, sent)
 
 
 def shards(layer_input, top_grad, gate_weight, up_weight, down_weight, activity):
-    sent, x_all, dy_all, hid, gh, gu = relay_call(
+    sent, xt, dy_all, hid, gh, gu = relay_call(
         layer_input, top_grad, gate_weight, up_weight, down_weight, activity
     )
     flat = lambda a: a.reshape(2 * TOK, a.shape[-1])
-    return weights_call(flat(x_all), flat(dy_all), flat(hid), flat(gh), flat(gu), sent)
+    return weights_call(xt, flat(dy_all), flat(hid), flat(gh), flat(gu), sent)
 
 
 def solution(mesh):

time: 85.5 us -> 83.6 us (0.978)
  Pallas kernels: 84.7 us -> 82.8 us
    pallas_call x1, Pallas kernels: 78.1 us -> 76.5 us  [relay_call(): pl.pallas_call(functools.partial(relay_kernel, plans), name='relay', out_...]
where the time goes in v3:
time: 83.6 us; the launch traced here: 83.5 us
  Pallas kernels  82.8 us (99%)
    pallas_call x1, Pallas kernels, relay_call(): pl.pallas_call(functools.partial(relay_kernel, plans), name='relay', out_...  76.5 us
    pallas_call x1, Pallas kernels, weights_call(): pl.pallas_call(weights_kernel, name='weight_grads', grid=(FL // 256,), ou...  6.31 us

profile of v3, /device:TPU:1, one launch (start us, length us, event | category | flops | bytes accessed | tf_op | source)
XLA Modules:
  0.0 83.5 jit_solution(813215023553463730)
XLA Ops:
  0.6 76.5 %relay.1 = (bf16[1,2,16,1024]{3,2,1,0:T(8,128)(2,1)S(1)}, bf16[1024,256]{1,0:T(8,128)(2,1)S(1)}, bf16[2,128,1024]{2,1,0:T(8,128)(2,1)S(1)}, bf16[2,128,1792]{2,1...) custom-call(bf16[1,2,16,1024]{3,2,1,0:T(8,128)(2,1)} %x_hbm.1, ...), custom_call_target="tpu_custom_call" | custom-call | flops 5368709120 | bytes 16777216 | tf_op jit(solution)/shard_map/relay/pallas_call | solution.py:451
  77.2 6.3 %weight_grads.1 = (bf16[1,2,16,1024]{3,2,1,0:T(8,128)(2,1)}, bf16[1,1024,1792]{2,1,0:T(8,128)(2,1)}, bf16[1,1024,1792]{2,1,0:T(8,128)(2,1)}, bf16[1,1792,1024]{2,1,0:T(8,128)(2,1)}) custom-call(bf16[1024,256]{1,0:T(8,128)(2,1)S(1)} %get-tuple-element.10.xt_ref, bf16[256,1024]{1,0:T(8,128)(2,1)S(1)} %bitcast.7, bf16[256,1792]{1,0:T(8,128)(2,1)S(1)} %bitcast.4, ...), custom_call_target="tpu_custom_call" | custom-call | tf_op jit(solution)/shard_map/weight_grads/pallas_call | solution.py:508

commit v4 on v3

--- a/solution.py
+++ b/solution.py
@@ -25,9 +25,9 @@
 def relay_kernel(
     plans,
     x_hbm, top_hbm, wg_hbm, wu_hbm, wd_hbm, act_hbm,
-    sent_hbm, xt_hbm, dyall_hbm, hid_hbm, gh_hbm, gu_hbm,
+    sent_ref, xt_hbm, dyall_hbm, hid_hbm, gh_hbm, gu_hbm,
     xs, xt, dys, wg, wu, wd, wgt, wut, wdt, dn, ps, pr, yo, ys, yr,
-    agb0, agb1, agh0, agh1, hid, gh, gu, dxf, dxs, rr, sentv, act_ref, inv_y, inv_i,
+    agb0, agb1, agh0, agh1, hid, gh, gu, dxf, dxs, rr, act_ref, inv_y, inv_i,
     w_sem, own_sem, out_sem,
     x_s, x_r, dy_s, dy_r, pair_s, pair_r, y_s, y_r,
     ag_s, ag_r, agp_s, agp_r, hg_s, hg_r, hgp_s, hgp_r, rs_s, rs_r, hand_s, hand_r,
@@ -360,13 +360,12 @@
                 total = dys[m, rows16(col), cols].astype(F32) + dxf[m, half, rows16(col), :]
                 for i in range(7):
                     total = total + rr[m, half, i].astype(F32)
-                sentv[m, :, cols] = total.astype(BF16)
+                sent_ref[0, m, :, cols] = total.astype(BF16)
                 if is_last:
                     start(
-                        ("hand", m, half), sentv.at[m, :, halves[half]], dys.at[m, rows16(col), halves[half]],
+                        ("hand", m, half), sent_ref.at[0, m, :, halves[half]], dys.at[m, rows16(col), halves[half]],
                         hand_s.at[m, half], hand_r.at[m, half], relay,
                     )
-            start_local((5, m), sentv.at[m], sent_hbm.at[0, m], out_sem.at[5, m])
 
         def turn():
             for i, (src, dst) in enumerate(((wg, wgt), (wu, wut))):
@@ -399,12 +398,18 @@
             expand(m, (lambda a, b, c: agh[m][a, b, c],), (hid,))
             start_local((2, m), hid.at[m], hid_hbm.at[m], out_sem.at[2, m])
 
+        def drain():
+            for key in [key for key in sends if key[:2] != ("rs", 1)]:
+                sends.pop(key).wait_send()
+            for key in list(local):
+                local.pop(key).wait()
+
         for m in expected:
             for half in range(2):
                 block = dys.at[m, rows16(dy_block(col)), halves[half]]
                 recvs["hand", m, half] = remote(block, block, hand_s.at[m, half], hand_r.at[m, half], relay)
         table = dict(
-            ax=spread_x, ady=spread_top, wx=wait_x, inv=invert, turn=turn, gu=gate_up, gs=gate_sums, hs=spread_hidden, xt=turn_x, bk=back, rp=reduce_pair, act=activate, fwd=forward_grads, ex=expand_grads,
+            ax=spread_x, ady=spread_top, wx=wait_x, inv=invert, turn=turn, gu=gate_up, gs=gate_sums, hs=spread_hidden, xt=turn_x, drain=drain, bk=back, rp=reduce_pair, act=activate, fwd=forward_grads, ex=expand_grads,
             dx=input_grad, fin=finish, hid=hidden, dy=take_dy,
         )
         for name, *where in plan:
@@ -438,7 +443,7 @@
     ("ax", 0), ("ax", 1), ("inv",), ("turn",), ("wx", 0), ("gu", 0), ("wx", 1), ("gu", 1), ("rp", 0, 0), ("rp", 1, 0),
     ("gs", 0), ("hs", 0), ("gs", 1), ("hs", 1), ("xt",), ("hid", 0), ("hid", 1), ("dy", 0), ("bk", 0), ("rp", 0, 1),
     ("dy", 1), ("act", 0), ("bk", 1), ("rp", 1, 1), ("fwd", 0), ("ex", 0), ("act", 1), ("dx", 0), ("fwd", 1),
-    ("ex", 1), ("fin", 0), ("dx", 1), ("fin", 1),
+    ("ex", 1), ("fin", 0), ("dx", 1), ("drain",), ("fin", 1),
 )
 
 
@@ -460,7 +465,7 @@
             jax.ShapeDtypeStruct((2, TOK, FL), BF16),
         ),
         in_specs=[hbm] * 6,
-        out_specs=(any_space,) * 6,
+        out_specs=(pl.BlockSpec(memory_space=pltpu.VMEM),) + (any_space,) * 5,
         scratch_shapes=[
             vm((2, TOK, DL), BF16), vm((DL, 2 * TOK), BF16), vm((2, TOK, DL), BF16),
             vm((DL, FL), BF16), vm((DL, FL), BF16), vm((FL, DL), BF16),
@@ -472,7 +477,6 @@
             vm((5, 2) + tile, BF16), vm((5, 2) + tile, BF16),
             vm((2, TOK, FL), BF16), vm((2, TOK, FL), BF16), vm((2, TOK, FL), BF16),
             vm((2, 2, TOK, DL // 2), F32), vm((2, 2, TOK, DL // 2), BF16), vm((2, 2, 7, 16, DL // 2), BF16),
-            vm((2, 16, DL), BF16),
             pltpu.SMEM((1, 2, 2, 1, SLOTS), jnp.int32),
             pltpu.SMEM((2, 2, NBLK), jnp.int32), pltpu.SMEM((2, 2, NBLK), jnp.int32),
             dma((3,)), dma((5,)), dma((6, 2)),
@@ -498,9 +502,9 @@
         out_sent[...] = sent_ref[...]
 
     cut = pl.ds(pl.multiple_of(pl.program_id(0) * 256, 256), 256)
-    og[0] = jnp.dot(xt_ref[...], gh_ref[:, cut], preferred_element_type=F32).astype(BF16)
-    ou[0] = jnp.dot(xt_ref[...], gu_ref[:, cut], preferred_element_type=F32).astype(BF16)
-    od[0] = lax.dot_general(hid_ref[:, cut], dy_ref[...], TN, preferred_element_type=F32).astype(BF16)
+    og[0] = jnp.dot(xt_ref[cut, :], gh_ref[...], preferred_element_type=F32).astype(BF16)
+    ou[0] = jnp.dot(xt_ref[cut, :], gu_ref[...], preferred_element_type=F32).astype(BF16)
+    od[0] = lax.dot_general(hid_ref[...], dy_ref[:, cut], TN, preferred_element_type=F32).astype(BF16)
 
 
 def weights_call(xt, dy_all, hid, gh, gu, sent):
@@ -508,7 +512,7 @@
     return pl.pallas_call(
         weights_kernel,
         name="weight_grads",
-        grid=(FL // 256,),
+        grid=(DL // 256,),
         out_shape=(
             jax.ShapeDtypeStruct((1, 2, 16, DL), BF16),
             jax.ShapeDtypeStruct((1, DL, FL), BF16),
@@ -518,9 +522,9 @@
         in_specs=[pl.BlockSpec(memory_space=pltpu.VMEM)] * 6,
         out_specs=(
             whole((1, 2, 16, DL)),
-            pl.BlockSpec((1, DL, 256), lambda j: (0, 0, j)),
-            pl.BlockSpec((1, DL, 256), lambda j: (0, 0, j)),
-            pl.BlockSpec((1, 256, DL), lambda j: (0, j, 0)),
+            pl.BlockSpec((1, 256, FL), lambda j: (0, j, 0)),
+            pl.BlockSpec((1, 256, FL), lambda j: (0, j, 0)),
+            pl.BlockSpec((1, FL, 256), lambda j: (0, 0, j)),
         ),
         compiler_params=pltpu.CompilerParams(
             dimension_semantics=("arbitrary",), vmem_limit_bytes=24 * 2**20

time: 83.6 us -> 82.3 us (0.984)
  Pallas kernels: 82.8 us -> 81.5 us
    pallas_call x1, Pallas kernels: 6.31 us -> 5.27 us  [weights_call(): pl.pallas_call(weights_kernel, name='weight_grads', grid=(DL // 256,), ou...]
where the time goes in v4:
time: 82.3 us; the launch traced here: 82.2 us
  Pallas kernels  81.5 us (99%)
    pallas_call x1, Pallas kernels, relay_call(): pl.pallas_call(functools.partial(relay_kernel, plans), name='relay', out_...  76.2 us
    pallas_call x1, Pallas kernels, weights_call(): pl.pallas_call(weights_kernel, name='weight_grads', grid=(DL // 256,), ou...  5.27 us

profile of v4, /device:TPU:1, one launch (start us, length us, event | category | flops | bytes accessed | tf_op | source)
XLA Modules:
  0.0 82.2 jit_solution(3889318673524070835)
XLA Ops:
  0.6 76.2 %relay.1 = (bf16[1,2,16,1024]{3,2,1,0:T(8,128)(2,1)S(1)}, bf16[1024,256]{1,0:T(8,128)(2,1)S(1)}, bf16[2,128,1024]{2,1,0:T(8,128)(2,1)S(1)}, bf16[2,128,1792]{2,1...) custom-call(bf16[1,2,16,1024]{3,2,1,0:T(8,128)(2,1)} %x_hbm.1, ...), custom_call_target="tpu_custom_call" | custom-call | flops 5368709120 | bytes 16777216 | tf_op jit(solution)/shard_map/relay/pallas_call | solution.py:456
  76.9 5.3 %weight_grads.1 = (bf16[1,2,16,1024]{3,2,1,0:T(8,128)(2,1)}, bf16[1,1024,1792]{2,1,0:T(8,128)(2,1)}, bf16[1,1024,1792]{2,1,0:T(8,128)(2,1)}, bf16[1,1792,1024]{2,1,0:T(8,128)(2,1)}) custom-call(bf16[1024,256]{1,0:T(8,128)(2,1)S(1)} %get-tuple-element.10.xt_ref, bf16[256,1024]{1,0:T(8,128)(2,1)S(1)} %bitcast.7, bf16[256,1792]{1,0:T(8,128)(2,1)S(1)} %bitcast.4, ...), custom_call_target="tpu_custom_call" | custom-call | tf_op jit(solution)/shard_map/weight_grads/pallas_call | solution.py:512

commit v5 on v4

--- a/solution.py
+++ b/solution.py
@@ -10,7 +10,6 @@
 MESH = pl.DeviceIdType.MESH
 F32, BF16 = jnp.float32, jnp.bfloat16
 NT = (((1,), (1,)), ((), ()))
-TN = (((0,), (0,)), ((), ()))
 
 BLK = 64
 TOK = 128
@@ -27,7 +26,7 @@
     x_hbm, top_hbm, wg_hbm, wu_hbm, wd_hbm, act_hbm,
     sent_ref, xt_hbm, dyall_hbm, hid_hbm, gh_hbm, gu_hbm,
     xs, xt, dys, wg, wu, wd, wgt, wut, wdt, dn, ps, pr, yo, ys, yr,
-    agb0, agb1, agh0, agh1, hid, gh, gu, dxf, dxs, rr, act_ref, inv_y, inv_i,
+    agb0, agb1, agh0, agh1, hid, hidt, gh, gu, dxf, dxs, rr, act_ref, inv_y, inv_i,
     w_sem, own_sem, out_sem,
     x_s, x_r, dy_s, dy_r, pair_s, pair_r, y_s, y_r,
     ag_s, ag_r, agp_s, agp_r, hg_s, hg_r, hgp_s, hgp_r, rs_s, rs_r, hand_s, hand_r,
@@ -396,7 +395,9 @@
             for d in range(4):
                 arrived("hp", m, d)
             expand(m, (lambda a, b, c: agh[m][a, b, c],), (hid,))
-            start_local((2, m), hid.at[m], hid_hbm.at[m], out_sem.at[2, m])
+            hidt[:, TOK * m : TOK * m + TOK] = hid[m].T
+            if m == 1:
+                start_local((2, 0), hidt, hid_hbm, out_sem.at[2, 0])
 
         def drain():
             for key in [key for key in sends if key[:2] != ("rs", 1)]:
@@ -460,7 +461,7 @@
             jax.ShapeDtypeStruct((1, 2, 16, DL), BF16),
             jax.ShapeDtypeStruct((DL, 2 * TOK), BF16),
             jax.ShapeDtypeStruct((2, TOK, DL), BF16),
-            jax.ShapeDtypeStruct((2, TOK, FL), BF16),
+            jax.ShapeDtypeStruct((FL, 2 * TOK), BF16),
             jax.ShapeDtypeStruct((2, TOK, FL), BF16),
             jax.ShapeDtypeStruct((2, TOK, FL), BF16),
         ),
@@ -475,7 +476,7 @@
             vm((2, 3) + tile, F32), vm((2, 3, 3) + tile, BF16), vm((2, 3, 3) + tile, BF16),
             vm((5, 2, 2) + tile, BF16), vm((5, 2, 2) + tile, BF16),
             vm((5, 2) + tile, BF16), vm((5, 2) + tile, BF16),
-            vm((2, TOK, FL), BF16), vm((2, TOK, FL), BF16), vm((2, TOK, FL), BF16),
+            vm((2, TOK, FL), BF16), vm((FL, 2 * TOK), BF16), vm((2, TOK, FL), BF16), vm((2, TOK, FL), BF16),
             vm((2, 2, TOK, DL // 2), F32), vm((2, 2, TOK, DL // 2), BF16), vm((2, 2, 7, 16, DL // 2), BF16),
             pltpu.SMEM((1, 2, 2, 1, SLOTS), jnp.int32),
             pltpu.SMEM((2, 2, NBLK), jnp.int32), pltpu.SMEM((2, 2, NBLK), jnp.int32),
@@ -504,7 +505,7 @@
     cut = pl.ds(pl.multiple_of(pl.program_id(0) * 256, 256), 256)
     og[0] = jnp.dot(xt_ref[cut, :], gh_ref[...], preferred_element_type=F32).astype(BF16)
     ou[0] = jnp.dot(xt_ref[cut, :], gu_ref[...], preferred_element_type=F32).astype(BF16)
-    od[0] = lax.dot_general(hid_ref[...], dy_ref[:, cut], TN, preferred_element_type=F32).astype(BF16)
+    od[0] = jnp.dot(hid_ref[...], dy_ref[:, cut], preferred_element_type=F32).astype(BF16)
 
 
 def weights_call(xt, dy_all, hid, gh, gu, sent):
@@ -537,7 +538,7 @@
         layer_input, top_grad, gate_weight, up_weight, down_weight, activity
     )
     flat = lambda a: a.reshape(2 * TOK, a.shape[-1])
-    return weights_call(xt, flat(dy_all), flat(hid), flat(gh), flat(gu), sent)
+    return weights_call(xt, flat(dy_all), hid, flat(gh), flat(gu), sent)
 
 
 def solution(mesh):

time: 82.3 us -> 82.3 us (level)
  no operation moved by 1% of the time
where the time goes in v5:
time: 82.3 us; the launch traced here: 82.2 us
  Pallas kernels  81.6 us (99%)
    pallas_call x1, Pallas kernels, relay_call(): pl.pallas_call(functools.partial(relay_kernel, plans), name='relay', out_...  76.3 us
    pallas_call x1, Pallas kernels, weights_call(): pl.pallas_call(weights_kernel, name='weight_grads', grid=(DL // 256,), ou...  5.26 us

profile of v5, /device:TPU:1, one launch (start us, length us, event | category | flops | bytes accessed | tf_op | source)
XLA Modules:
  0.0 82.2 jit_solution(16376645332398659589)
XLA Ops:
  0.6 76.3 %relay.1 = (bf16[1,2,16,1024]{3,2,1,0:T(8,128)(2,1)S(1)}, bf16[1024,256]{1,0:T(8,128)(2,1)S(1)}, bf16[2,128,1024]{2,1,0:T(8,128)(2,1)S(1)}, bf16[1792,256]{1,0:T...) custom-call(bf16[1,2,16,1024]{3,2,1,0:T(8,128)(2,1)} %x_hbm.1, ...), custom_call_target="tpu_custom_call" | custom-call | flops 5368709120 | bytes 16777216 | tf_op jit(solution)/shard_map/relay/pallas_call | solution.py:457
  76.9 5.3 %weight_grads.1 = (bf16[1,2,16,1024]{3,2,1,0:T(8,128)(2,1)}, bf16[1,1024,1792]{2,1,0:T(8,128)(2,1)}, bf16[1,1024,1792]{2,1,0:T(8,128)(2,1)}, bf16[1,1792,1024]{2,1,0:T(8,128)(2,1)}) custom-call(bf16[1024,256]{1,0:T(8,128)(2,1)S(1)} %get-tuple-element.10.xt_ref, bf16[256,1024]{1,0:T(8,128)(2,1)S(1)} %bitcast.5, ...), custom_call_target="tpu_custom_call" | custom-call | tf_op jit(solution)/shard_map/weight_grads/pallas_call | solution.py:513
